TPU v7x, 128 devices: a whole 4x4x4 slice. The times are simulated.
128 devices in a mesh: region: 32 (over x, y, core), grp: 4 (over z).
Axes of the slice: x: 4, y: 4, z: 4, core: 2. Of those that a mesh axis runs over, the one named last changes fastest.
Arguments:
- ensemble: float32 [80, 16, 65536], P('grp', None, 'region')
- loc_weight: bfloat16 [8, 65536, 256], P(None, ('region', 'grp')), may hold values from 0.019897461 to 0.5
- obs_value: float32 [8, 256], replicated, may hold values from -6 to 6
- obs_var: float32 [8, 256], replicated, may hold values from 0.1 to 1
- owner_region: int32 [8], replicated, may hold values from 0 to 31
- obs_cell: int32 [8, 256], replicated, may hold values from 0 to 32767
- batch_order: int32 [8], replicated, may hold values from 0 to 7, each once
Outputs:
- analysis: float32 [80, 16, 65536], P('grp', None, 'region')
Inputs may be any that keep to these rules, and one draw needn't show every extreme that they name: `batch_order`: each batch index appears once.
All inputs are finite; a program needn't handle non-finite values.
Results may differ from a plain program's by a relative error of at most 0.0003.
Values sent between devices are 32-bit elements; how exact they have to be, the bound alone decides.
A program may use at most 128 MiB of HBM per device.

v0:
```python
import jax
import jax.numpy as jnp
from jax import lax
from jax.sharding import PartitionSpec as P

epsilon = 1e-05


def spread_2(value, axis, source):
    kept = jnp.where(lax.axis_index(axis) == source, value, 0).astype(value.dtype)
    return lax.psum(kept, axis)


def statistics(prior_obs):
    members = prior_obs.shape[0]
    centre = jnp.mean(prior_obs, 0)
    obs_anom = prior_obs - centre
    spread = jnp.sum(obs_anom * obs_anom, 0) / (members - 1) + epsilon
    return (centre, obs_anom, spread)


def adjust(prior_obs, centre, obs_anom, spread, values, variance):
    denom_sum = spread + variance
    post_centre = (variance * centre + spread * values) / denom_sum
    factor = jnp.sqrt(variance / denom_sum)
    return post_centre + factor * obs_anom - prior_obs


def regress(state_blk, weights_blk, obs_anom, change, spread):
    members = state_blk.shape[0]
    width = weights_blk.shape[0]
    centre = jnp.mean(state_blk, 0)
    state_anom = (state_blk - centre).reshape(members, -1)
    covariance = lax.dot_general(
        state_anom, obs_anom, (((0,), (0,)), ((), ())), precision=lax.Precision.HIGHEST
    )
    inverse_var = 1.0 / ((members - 1) * spread)
    kalman_gain = (
        covariance.reshape(-1, width, obs_anom.shape[1])
        * weights_blk.astype(jnp.float32)[None]
        * inverse_var
    )
    kalman_gain = kalman_gain.reshape(-1, obs_anom.shape[1])
    increment = lax.dot_general(
        change, kalman_gain, (((1,), (1,)), ((), ())), precision=lax.Precision.HIGHEST
    )
    return state_blk + increment.reshape(state_blk.shape)


def body(ensemble, loc_weight, obs_value, obs_var, owner_region, obs_cell, batch_order):
    state = lax.all_to_all(ensemble, "grp", split_axis=2, concat_axis=0, tiled=True)
    members, stack, cols_dev = state.shape
    cols_reg = cols_dev * lax.axis_size("grp")
    here_region = lax.axis_index("region")
    here_group = lax.axis_index("grp")
    for turn in range(batch_order.shape[0]):
        batch = batch_order[turn]
        region_id = owner_region[batch]
        cell_ids = obs_cell[batch]
        level_idx = cell_ids // cols_reg
        local_col = cell_ids % cols_reg - here_group * cols_dev
        inside = (region_id == here_region) & (local_col >= 0) & (local_col < cols_dev)
        flat_idx = level_idx * cols_dev + jnp.clip(local_col, 0, cols_dev - 1)
        picked = jnp.take(state.reshape(members, stack * cols_dev), flat_idx, axis=1)
        masked = jnp.where(inside[None, :], picked, jnp.float32(0.0))
        values_now = obs_value[batch]
        variance_now = obs_var[batch]
        summed = lax.psum(masked, "grp")
        centre, obs_anom, spread = statistics(summed)
        sent_change = adjust(summed, centre, obs_anom, spread, values_now, variance_now)
        prior_obs, change = (
            spread_2(summed, "region", region_id),
            spread_2(sent_change, "region", region_id),
        )
        centre, obs_anom, spread = statistics(prior_obs)
        state = regress(state, loc_weight[batch], obs_anom, change, spread)
    return lax.all_to_all(state, "grp", split_axis=0, concat_axis=2, tiled=True)


def solution(mesh):
    return jax.shard_map(
        body,
        mesh=mesh,
        in_specs=(
            P("grp", None, "region"),
            P(None, ("region", "grp"), None),
            P(),
            P(),
            P(),
            P(),
            P(),
        ),
        out_specs=P("grp", None, "region"),
        check_vma=False,
    )
```

profile of v0, /device:TPU:1, one launch (start us, length us, event | category | flops | bytes accessed | tf_op | source)
XLA Modules:
  0.0 1528.3 jit_solution(3187241296763926514)
XLA Ops:
  6.5 12.4 copy.139
  18.9 21.9 %reshape.537 = f32[4,1,163840]{2,1,0:T(1,128)} reshape(f32[2048,16,20]{2,1,0:T(8,128)} %bitcast.293) | data formatting | bytes 5242880
  78.5 9.7 reduce.17
  88.2 27.0 %reshape.538 = f32[2048,16,20]{2,1,0:T(8,128)} reshape(f32[4,163840]{1,0:T(4,128)} %reduce.17) | data formatting | bytes 5242880
  115.2 10.8 copy.184
  135.9 39.3 %all-reduce.25.cloned.1.call-done = f32[80,256]{1,0:T(8,128)} async-done(((f32[80,256]{1,0:T(8,128)}), f32[80,256]{1,0:T(8,128)}) %all-reduce.25.cloned.1.call-update) | async-done | bytes 81936 | tf_op jit(solution)/shard_map/psum | solution.py:68
  178.7 8.8 all-reduce.27.cloned.1.call-start
  189.2 90.7 %all-reduce.55.cloned.1.call-done = (f32[80,256]{1,0:T(8,128)}, f32[80,256]{1,0:T(8,128)}) async-done(((f32[80,256]{1,0:T(8,128)}, f32[80,256]{1,0:T(8,128)}), (f32[80,256]{1,0:T(8,128)}, f32[80,256]{1,0:T(8,128)})) %all-reduce.55.cloned.1.call-update) | async-done | bytes 163856 | tf_op jit(solution)/shard_map/psum | solution.py:11
  281.8 8.8 fusion.61
  290.6 9.3 fusion.169
  307.1 37.7 %all-reduce.27.cloned.1.call-done = f32[80,256]{1,0:T(8,128)} async-done(((f32[80,256]{1,0:T(8,128)}), f32[80,256]{1,0:T(8,128)}) %all-reduce.27.cloned.1.call-update) | async-done | bytes 81936 | tf_op jit(solution)/shard_map/psum | solution.py:68
  348.3 101.1 %all-reduce.53.cloned.1.call-done = (f32[80,256]{1,0:T(8,128)}, f32[80,256]{1,0:T(8,128)}) async-done(((f32[80,256]{1,0:T(8,128)}, f32[80,256]{1,0:T(8,128)}), (f32[80,256]{1,0:T(8,128)}, f32[80,256]{1,0:T(8,128)})) %all-reduce.53.cloned.1.call-update) | async-done | bytes 163856 | tf_op jit(solution)/shard_map/psum | solution.py:11
  459.2 9.7 fusion.170
  477.5 37.7 %all-reduce.29.cloned.1.call-done = f32[80,256]{1,0:T(8,128)} async-done(((f32[80,256]{1,0:T(8,128)}), f32[80,256]{1,0:T(8,128)}) %all-reduce.29.cloned.1.call-update) | async-done | bytes 81936 | tf_op jit(solution)/shard_map/psum | solution.py:68
  518.7 101.1 %all-reduce.51.cloned.1.call-done = (f32[80,256]{1,0:T(8,128)}, f32[80,256]{1,0:T(8,128)}) async-done(((f32[80,256]{1,0:T(8,128)}, f32[80,256]{1,0:T(8,128)}), (f32[80,256]{1,0:T(8,128)}, f32[80,256]{1,0:T(8,128)})) %all-reduce.51.cloned.1.call-update) | async-done | bytes 163856 | tf_op jit(solution)/shard_map/psum | solution.py:11
  629.8 8.4 fusion.171
  645.3 37.7 %all-reduce.31.cloned.1.call-done = f32[80,256]{1,0:T(8,128)} async-done(((f32[80,256]{1,0:T(8,128)}), f32[80,256]{1,0:T(8,128)}) %all-reduce.31.cloned.1.call-update) | async-done | bytes 81936 | tf_op jit(solution)/shard_map/psum | solution.py:68
  686.6 101.2 %all-reduce.49.cloned.1.call-done = (f32[80,256]{1,0:T(8,128)}, f32[80,256]{1,0:T(8,128)}) async-done(((f32[80,256]{1,0:T(8,128)}, f32[80,256]{1,0:T(8,128)}), (f32[80,256]{1,0:T(8,128)}, f32[80,256]{1,0:T(8,128)})) %all-reduce.49.cloned.1.call-update) | async-done | bytes 163856 | tf_op jit(solution)/shard_map/psum | solution.py:11
  797.6 9.7 fusion.172
  815.9 37.7 %all-reduce.33.cloned.1.call-done = f32[80,256]{1,0:T(8,128)} async-done(((f32[80,256]{1,0:T(8,128)}), f32[80,256]{1,0:T(8,128)}) %all-reduce.33.cloned.1.call-update) | async-done | bytes 81936 | tf_op jit(solution)/shard_map/psum | solution.py:68
  857.1 101.0 %all-reduce.47.cloned.1.call-done = (f32[80,256]{1,0:T(8,128)}, f32[80,256]{1,0:T(8,128)}) async-done(((f32[80,256]{1,0:T(8,128)}, f32[80,256]{1,0:T(8,128)}), (f32[80,256]{1,0:T(8,128)}, f32[80,256]{1,0:T(8,128)})) %all-reduce.47.cloned.1.call-update) | async-done | bytes 163856 | tf_op jit(solution)/shard_map/psum | solution.py:11
  968.2 8.4 fusion.173
  983.7 37.7 %all-reduce.35.cloned.1.call-done = f32[80,256]{1,0:T(8,128)} async-done(((f32[80,256]{1,0:T(8,128)}), f32[80,256]{1,0:T(8,128)}) %all-reduce.35.cloned.1.call-update) | async-done | bytes 81936 | tf_op jit(solution)/shard_map/psum | solution.py:68
  1025.0 101.1 %all-reduce.45.cloned.1.call-done = (f32[80,256]{1,0:T(8,128)}, f32[80,256]{1,0:T(8,128)}) async-done(((f32[80,256]{1,0:T(8,128)}, f32[80,256]{1,0:T(8,128)}), (f32[80,256]{1,0:T(8,128)}, f32[80,256]{1,0:T(8,128)})) %all-reduce.45.cloned.1.call-update) | async-done | bytes 163856 | tf_op jit(solution)/shard_map/psum | solution.py:11
  1135.9 9.7 fusion.174
  1154.1 37.7 %all-reduce.37.cloned.1.call-done = f32[80,256]{1,0:T(8,128)} async-done(((f32[80,256]{1,0:T(8,128)}), f32[80,256]{1,0:T(8,128)}) %all-reduce.37.cloned.1.call-update) | async-done | bytes 81936 | tf_op jit(solution)/shard_map/psum | solution.py:68
  1195.4 101.1 %all-reduce.43.cloned.1.call-done = (f32[80,256]{1,0:T(8,128)}, f32[80,256]{1,0:T(8,128)}) async-done(((f32[80,256]{1,0:T(8,128)}, f32[80,256]{1,0:T(8,128)}), (f32[80,256]{1,0:T(8,128)}, f32[80,256]{1,0:T(8,128)})) %all-reduce.43.cloned.1.call-update) | async-done | bytes 163856 | tf_op jit(solution)/shard_map/psum | solution.py:11
  1306.4 8.3 fusion.175
  1322.5 37.1 %all-reduce.39.cloned.1.call-done = f32[80,256]{1,0:T(8,128)} async-done(((f32[80,256]{1,0:T(8,128)}), f32[80,256]{1,0:T(8,128)}) %all-reduce.39.cloned.1.call-update) | async-done | bytes 81936 | tf_op jit(solution)/shard_map/psum | solution.py:68
  1363.0 101.1 %all-reduce.41.cloned.1.call-done = (f32[80,256]{1,0:T(8,128)}, f32[80,256]{1,0:T(8,128)}) async-done(((f32[80,256]{1,0:T(8,128)}, f32[80,256]{1,0:T(8,128)}), (f32[80,256]{1,0:T(8,128)}, f32[80,256]{1,0:T(8,128)})) %all-reduce.41.cloned.1.call-update) | async-done | bytes 163856 | tf_op jit(solution)/shard_map/psum | solution.py:11
  1473.9 8.4 fusion.84
  1483.9 35.7 %all_to_all.36 = f32[80,16,512]{2,1,0:T(8,128)S(1)} all-to-all(f32[80,16,512]{2,1,0:T(8,128)S(1)} %copy.182), channel_id=1, replica_groups=mesh['region'=32,'grp'=4] {'grp'}, dimensions={0} | all-to-all | bytes 5242880 | tf_op jit(solution)/shard_map/all_to_all | solution.py:77
  (240 shorter events, 180.7 us)
Async XLA Ops:
  40.9 21.7 %copy-start.23 = (s32[8]{0:T(128)S(1)}, s32[8]{0:T(128)}, u32[]{:S(2)}) copy-start(s32[8]{0:T(128)} %param.13) | copy-start | bytes 100
  40.9 31.7 %copy-start.25 = (s32[8,256]{1,0:T(8,128)S(1)}, s32[8,256]{1,0:T(8,128)}, u32[]{:S(2)}) copy-start(s32[8,256]{1,0:T(8,128)} %param.14) | copy-start | bytes 24580
  40.9 37.0 %all-to-all-start = ((f32[4,1,163840]{2,1,0:T(1,128)}), f32[4,1,163840]{2,1,0:T(1,128)S(1)}, u32[]{:S(2)}, u32[]{:S(2)}) async-start(f32[4,1,163840]{2,1,0:T(1,128)} %reshape.537), calls=%async_computation | async-start | bytes 5242880 | tf_op jit(solution)/shard_map/all_to_all | solution.py:51
  46.9 128.3 %all-reduce.25.cloned.1.call-start = ((), (), s32[]{:S(2)}) async-start(), calls=%async_computation.2 | async-start | bytes 163840 | tf_op jit(solution)/shard_map/psum | solution.py:68
  128.9 48.2 %copy-start.26 = (f32[8,256]{1,0:T(8,128)S(1)}, f32[8,256]{1,0:T(8,128)}, u32[]{:S(2)}) copy-start(f32[8,256]{1,0:T(8,128)} %param.11) | copy-start | bytes 24580
  128.9 48.2 %copy-start.27 = (f32[8,256]{1,0:T(8,128)S(1)}, f32[8,256]{1,0:T(8,128)}, u32[]{:S(2)}) copy-start(f32[8,256]{1,0:T(8,128)} %param.12) | copy-start | bytes 24580
  135.9 144.1 %all-reduce.55.cloned.1.call-start = ((), (), s32[]{:S(2)}) async-start(), calls=%async_computation.17 | async-start | bytes 327680 | tf_op jit(solution)/shard_map/psum | solution.py:11
  178.7 166.1 %all-reduce.27.cloned.1.call-start = ((), (), s32[]{:S(2)}) async-start(), calls=%async_computation.3 | async-start | bytes 163840 | tf_op jit(solution)/shard_map/psum | solution.py:68
  281.8 8.8 copy-start.7
  281.8 8.8 copy-start.14
  281.8 8.8 copy-start.15
  307.0 142.4 %all-reduce.53.cloned.1.call-start = ((), (), s32[]{:S(2)}) async-start(), calls=%async_computation.16 | async-start | bytes 327680 | tf_op jit(solution)/shard_map/psum | solution.py:11
  348.2 166.9 %all-reduce.29.cloned.1.call-start = ((), (), s32[]{:S(2)}) async-start(), calls=%async_computation.4 | async-start | bytes 163840 | tf_op jit(solution)/shard_map/psum | solution.py:68
  468.9 152.7 %copy-start = (f32[80,16,512]{2,0,1:T(8,128)S(1)}, f32[80,16,512]{2,0,1:T(8,128)}, u32[]{:S(2)}) copy-start(f32[80,16,512]{2,0,1:T(8,128)} %get-tuple-element.127) | copy-start | bytes 7864324
  477.4 142.4 %all-reduce.51.cloned.1.call-start = ((), (), s32[]{:S(2)}) async-start(), calls=%async_computation.15 | async-start | bytes 327680 | tf_op jit(solution)/shard_map/psum | solution.py:11
  518.6 164.4 %all-reduce.31.cloned.1.call-start = ((), (), s32[]{:S(2)}) async-start(), calls=%async_computation.5 | async-start | bytes 163840 | tf_op jit(solution)/shard_map/psum | solution.py:68
  621.6 8.1 copy-start.1
  645.2 142.5 %all-reduce.49.cloned.1.call-start = ((), (), s32[]{:S(2)}) async-start(), calls=%async_computation.14 | async-start | bytes 327680 | tf_op jit(solution)/shard_map/psum | solution.py:11
  686.5 167.1 %all-reduce.33.cloned.1.call-start = ((), (), s32[]{:S(2)}) async-start(), calls=%async_computation.6 | async-start | bytes 163840 | tf_op jit(solution)/shard_map/psum | solution.py:68
  807.3 152.7 %copy-start.2 = (f32[80,16,512]{2,0,1:T(8,128)S(1)}, f32[80,16,512]{2,0,1:T(8,128)}, u32[]{:S(2)}) copy-start(f32[80,16,512]{2,0,1:T(8,128)} %get-tuple-element.131) | copy-start | bytes 7864324
  815.8 142.4 %all-reduce.47.cloned.1.call-start = ((), (), s32[]{:S(2)}) async-start(), calls=%async_computation.13 | async-start | bytes 327680 | tf_op jit(solution)/shard_map/psum | solution.py:11
  857.1 164.3 %all-reduce.35.cloned.1.call-start = ((), (), s32[]{:S(2)}) async-start(), calls=%async_computation.7 | async-start | bytes 163840 | tf_op jit(solution)/shard_map/psum | solution.py:68
  960.0 8.1 copy-start.3
  983.7 142.4 %all-reduce.45.cloned.1.call-start = ((), (), s32[]{:S(2)}) async-start(), calls=%async_computation.12 | async-start | bytes 327680 | tf_op jit(solution)/shard_map/psum | solution.py:11
  1024.9 167.0 %all-reduce.37.cloned.1.call-start = ((), (), s32[]{:S(2)}) async-start(), calls=%async_computation.8 | async-start | bytes 163840 | tf_op jit(solution)/shard_map/psum | solution.py:68
  1145.6 152.7 %copy-start.4 = (f32[80,16,512]{2,0,1:T(8,128)S(1)}, f32[80,16,512]{2,0,1:T(8,128)}, u32[]{:S(2)}) copy-start(f32[80,16,512]{2,0,1:T(8,128)} %get-tuple-element.135) | copy-start | bytes 7864324
  1154.1 142.4 %all-reduce.43.cloned.1.call-start = ((), (), s32[]{:S(2)}) async-start(), calls=%async_computation.11 | async-start | bytes 327680 | tf_op jit(solution)/shard_map/psum | solution.py:11
  1195.3 164.2 %all-reduce.39.cloned.1.call-start = ((), (), s32[]{:S(2)}) async-start(), calls=%async_computation.9 | async-start | bytes 163840 | tf_op jit(solution)/shard_map/psum | solution.py:68
  1298.3 8.1 copy-start.5
  1298.3 8.1 copy-start.8
  1298.3 8.1 copy-start.21
  1321.7 142.4 %all-reduce.41.cloned.1.call-start = ((), (), s32[]{:S(2)}) async-start(), calls=%async_computation.10 | async-start | bytes 327680 | tf_op jit(solution)/shard_map/psum | solution.py:11
  (13 other events, 96.2 us)
Sparse Core Ops, SparseCore 0:
  136.0 39.1 all-reduce.24
  178.9 100.9 all-reduce.54
  307.1 37.5 all-reduce.26
  348.4 100.9 all-reduce.52
  477.5 37.5 all-reduce.28
  518.8 100.9 all-reduce.50
  645.4 37.6 all-reduce.30
  686.8 100.9 all-reduce.48
  815.9 37.6 all-reduce.32
  857.2 100.9 all-reduce.46
  983.8 37.5 all-reduce.34
  1025.0 100.9 all-reduce.44
  1154.2 37.6 all-reduce.36
  1195.4 100.9 all-reduce.42
  1321.8 37.6 all-reduce.38
  1363.1 100.9 all-reduce.40
where the time goes:
time: 1540 us; the launch traced here: 1530 us
  waiting for transfers between devices  1100 us (71%)
  matrix products  137 us (9%)
  local copies, waits for them, and re-layouts  135 us (9%)
  other arithmetic  62.7 us (4%)
  between operations  39.6 us (3%)
  blocking collectives  35.7 us (2%)
  starting transfers between devices  15.4 us (1%)
    psum x8, waiting for transfers between devices, spread_2(): return lax.psum(kept, axis)  798 us
    psum x8, waiting for transfers between devices, body(): summed = lax.psum(masked, 'grp')  303 us
    dot_general x8, matrix products, regress(): lax.dot_general(change, kalman_gain, (((1,), (1,)), ((), ())), precision=...  71.9 us
    dot_general x8, matrix products, regress(): lax.dot_general(state_anom, obs_anom, (((0,), (0,)), ((), ())), precision...  64.9 us
    unnamed x61, local copies, waits for them, and re-layouts  63.1 us
    all_to_all x1, blocking collectives, body(): return lax.all_to_all(state, 'grp', split_axis=0, concat_axis=2, tiled=True)  35.7 us
    reshape x8, local copies, waits for them, and re-layouts, body(): state.reshape(members, stack * cols_dev)  31.3 us
  transfers between devices with their start and end apart: 17, of which 17 were waited for; matrix products, arithmetic and copies ran while one was open for 0% of the time, Pallas kernels for 0%

commit v1 on v0

v1 whole, which is shorter than its diff:
```python
import functools

import jax
import jax.numpy as jnp
from jax import lax
from jax.experimental import pallas as pl
from jax.experimental.pallas import tpu as pltpu
from jax.sharding import PartitionSpec as P

epsilon = 1e-05
MESH = pl.DeviceIdType.MESH
F32, BF16 = jnp.float32, jnp.bfloat16

TURNS, OBS, MEM, SLAB, STACK = 8, 256, 80, 20, 16
COLS_REG, COLS_DEV = 2048, 512
GROUP = 4
PAIRS = [(a, b) for h in (0, GROUP) for b in range(h, h + GROUP) for a in range(h, b)]
PAIR_ROW = {p: i * OBS for i, p in enumerate(PAIRS)}
CROSS = [(a, b) for b in range(GROUP, TURNS) for a in range(GROUP)]
CROSS_AT = {p: i for i, p in enumerate(CROSS)}
X0_ROW = len(PAIRS) * OBS
A_ROWS = 3840
D_ROWS = 384
CHUNKS, CHUNK = 4, 128
WIDE = 4


def split2(value):
    high = value.astype(BF16)
    low = (value - high.astype(F32)).astype(BF16)
    return high, low


def increment(x, left, change, weights):
    anom = x - jnp.sum(x, 0, keepdims=True) * (1.0 / MEM)
    high, low = split2(anom)
    stacked = jnp.concatenate([high, high, low], 0)
    gain = jnp.dot(left, stacked, preferred_element_type=F32) * weights
    g_high, g_low = split2(gain)
    first = jnp.dot(change, g_high, preferred_element_type=F32)
    second = jnp.dot(change[:MEM], g_low, preferred_element_type=F32)
    return first[:MEM] + first[MEM:] + second


def turn_operands(prior, value, variance):
    centre = jnp.sum(prior, 0, keepdims=True) * (1.0 / MEM)
    anom = prior - centre
    spread = jnp.sum(anom * anom, 0, keepdims=True) / (MEM - 1) + epsilon
    denom = spread + variance
    post = (variance * centre + spread * value) / denom
    factor = jnp.sqrt(variance / denom)
    change = post + factor * anom - prior
    scaled = anom * (1.0 / ((MEM - 1) * spread))
    high = scaled.astype(BF16).astype(F32)
    low = scaled - high
    left = jnp.concatenate([high, low, high], 0).T.astype(BF16)
    c_high, c_low = split2(change)
    return left, jnp.concatenate([c_high, c_low], 0)


def pick_kernel(order, owner, cells, ens, out, held, sem):
    here = lax.axis_index("region")
    out[...] = jnp.zeros_like(out)
    mine = [owner[order[t]] == here for t in range(TURNS)]
    some = functools.reduce(jnp.logical_or, mine)

    @pl.when(some)
    def _():
        copy = pltpu.make_async_copy(ens, held, sem)
        copy.start()
        copy.wait()

    for t in range(TURNS):

        @pl.when(mine[t])
        def _(t=t):
            cell = cells[pl.ds(order[t], 1), :]
            column = cell & (COLS_REG - 1)
            level = cell >> 11
            depth = 512

            def part(k, total):
                at = pl.multiple_of(k * depth, depth)
                rows = lax.broadcasted_iota(jnp.int32, (depth, OBS), 0) + at
                select = jnp.where(rows == column, 1.0, 0.0).astype(BF16)
                value = held[:, pl.ds(at, depth)]
                high = value.astype(BF16)
                rest = value - high.astype(F32)
                middle, low = split2(rest)
                for piece in (high, middle, low):
                    total = total + jnp.dot(piece, select, preferred_element_type=F32)
                return total

            total = lax.fori_loop(0, COLS_REG // depth, part, jnp.zeros((SLAB * STACK, OBS), F32))
            total = total.reshape(SLAB, STACK, OBS)
            levels = lax.broadcasted_iota(jnp.int32, (SLAB, STACK, OBS), 1)
            out[t, 0:SLAB, :] = jnp.sum(jnp.where(levels == level[None], total, 0.0), 1)


def places():
    region, z = lax.axis_index("region"), lax.axis_index("grp")
    return region // 8, (region // 2) % 4, region % 2, z


def peer(axis, k):
    x, y, c, z = places()
    if axis == "x":
        x = lax.rem(x + k, 4)
    elif axis == "y":
        y = lax.rem(y + k, 4)
    elif axis == "z":
        z = lax.rem(z + k, 4)
    else:
        c = 1 - c
    return (x * 8 + y * 2 + c, z)


def all_reduce(a, b, rows, sib, inbox, sib_sem, send, recv):
    x, y, c, z = places()
    at = {"x": x, "y": y, "z": z}
    axes = ("x", "y", "z")
    q = rows // 24
    t, h = 4 * q, 12 * q
    base, other = pl.multiple_of(c * h, 8), pl.multiple_of((1 - c) * h, 8)
    own = [pl.multiple_of(base + i * t + at[axes[i]] * q, 8) for i in range(3)]

    def remote(src, dst, s, r, device):
        return pltpu.make_async_remote_copy(src, dst, s, r, device_id=device, device_id_type=MESH)

    copy = remote(a.at[pl.ds(other, h)], sib, sib_sem.at[0], sib_sem.at[1], peer("c", 1))
    copy.start()
    copy.wait()
    a[pl.ds(base, h), :] += sib[...]
    for phase in range(3):
        copies = []
        for k in (1, 2, 3):
            for i in range(3):
                axis = axes[(i + phase) % 3]
                if phase == 0:
                    src = pl.multiple_of(base + i * t + lax.rem(at[axis] + k, 4) * q, 8)
                else:
                    src = own[i]
                copy = remote(a.at[pl.ds(src, q)], inbox.at[phase, i, k - 1], send.at[phase, i, k - 1],
                              recv.at[phase, i, k - 1], peer(axis, k))
                copy.start()
                copies.append(copy)
        for copy in copies:
            copy.wait()
        for i in range(3):
            into = b if phase == 2 else a
            into[pl.ds(own[i], q), :] = (
                a[pl.ds(own[i], q), :] + inbox[phase, i, 0] + inbox[phase, i, 1] + inbox[phase, i, 2])
    copies = []
    for k in (1, 2, 3):
        for i in range(3):
            rows_i = b.at[pl.ds(own[i], q)]
            copy = remote(rows_i, rows_i, send.at[3, i, k - 1], recv.at[3, i, k - 1], peer(axes[i], k))
            copy.start()
            copies.append(copy)
    for copy in copies:
        copy.wait()
    half = b.at[pl.ds(base, h)]
    copy = remote(half, half, sib_sem.at[2], sib_sem.at[3], peer("c", 1))
    copy.start()
    copy.wait()


def main_kernel(order, owner, cells, values, variances, weights, picked, ens, out,
                stage, outbox, a, a_sum, d, d_sum, wt, cross, prior, left, change, tile,
                sib_a, in_a, sib_d, in_d,
                go_send, go_recv, go_own, back_send, back_recv, back_own,
                sibsem_a, send_a, recv_a, sibsem_d, send_d, recv_d):
    region, z = lax.axis_index("region"), lax.axis_index("grp")

    barrier = pltpu.get_barrier_semaphore()
    around = [peer(axis, k) for axis in ("x", "y", "z") for k in (1, 2, 3)] + [peer("c", 1)]
    for device in around:
        pl.semaphore_signal(barrier, 1, device_id=device, device_id_type=MESH)
    pl.semaphore_wait(barrier, len(around))

    go = []
    for k in (1, 2, 3):
        to = lax.rem(z + k, 4)
        for q in range(CHUNKS):
            src = ens.at[:, pl.ds(pl.multiple_of(to * COLS_DEV + q * CHUNK, 128), CHUNK)]
            go.append(pltpu.make_async_remote_copy(
                src, stage.at[z, q], go_send.at[q, k - 1], go_recv.at[q, k - 1],
                device_id=peer("z", k), device_id_type=MESH))
    for q in range(CHUNKS):
        src = ens.at[:, pl.ds(pl.multiple_of(z * COLS_DEV + q * CHUNK, 128), CHUNK)]
        go.append(pltpu.make_async_copy(src, stage.at[z, q], go_own.at[q]))
    for copy in go:
        copy.start()

    for t in range(TURNS):
        wt[t] = weights[order[t]].astype(F32).T.astype(BF16)

    for b in range(TURNS):
        column = cells[pl.ds(order[b], 1), :] & (COLS_REG - 1)
        local = column - z * COLS_DEV
        local = jnp.where(owner[order[b]] == region, local, -1)
        select = jnp.where(lax.broadcasted_iota(jnp.int32, (COLS_DEV, OBS), 0) == local, 1.0, 0.0).astype(BF16)
        for t in range(b):
            rows = jnp.dot(wt[t], select, preferred_element_type=F32)
            if (t, b) in PAIR_ROW:
                a[PAIR_ROW[t, b]:PAIR_ROW[t, b] + OBS, :] = rows
            else:
                cross[CROSS_AT[t, b]] = rows.astype(BF16)
        for k in range(4):
            at = X0_ROW + b * MEM + k * SLAB
            a[at:at + SLAB, :] = jnp.where(z == k, picked[b, 0:SLAB, :], 0.0)
    a[X0_ROW + TURNS * MEM:A_ROWS, :] = jnp.zeros((A_ROWS - X0_ROW - TURNS * MEM, OBS), F32)
    d[...] = jnp.zeros_like(d)

    all_reduce(a, a_sum, A_ROWS, sib_a, in_a, sibsem_a, send_a, recv_a)

    for t in range(TURNS):
        prior[t] = a_sum[X0_ROW + t * MEM:X0_ROW + (t + 1) * MEM, :]

    for t in range(TURNS):
        if t == GROUP:
            all_reduce(d, d_sum, D_ROWS, sib_d, in_d, sibsem_d, send_d, recv_d)
            for b in range(GROUP, TURNS):
                at = (b - GROUP) * MEM
                prior[b] = a_sum[X0_ROW + b * MEM:X0_ROW + (b + 1) * MEM, :] + d_sum[at:at + MEM, :]
        left[t], change[t] = turn_operands(
            prior[t], values[pl.ds(order[t], 1), :], variances[pl.ds(order[t], 1), :])
        for b in range(t + 1, TURNS):
            if (t, b) in PAIR_ROW:
                row = PAIR_ROW[t, b]
                prior[b] += increment(prior[b], left[t], change[t], a_sum[row:row + OBS, :])
            else:
                at = (b - GROUP) * MEM
                step = increment(prior[b], left[t], change[t], cross[CROSS_AT[t, b]].astype(F32))
                d[at:at + MEM, :] += step
                prior[b] += step

    for copy in go:
        copy.wait()

    def send_back(q):
        there = pl.ds(pl.multiple_of(z * COLS_DEV + q * CHUNK, 128), CHUNK)
        for k in (1, 2, 3):
            to = lax.rem(z + k, 4)
            yield pltpu.make_async_remote_copy(
                outbox.at[to, q], out.at[:, there], back_send.at[q, k - 1], back_recv.at[q, k - 1],
                device_id=peer("z", k), device_id_type=MESH)
        yield pltpu.make_async_copy(outbox.at[z, q], out.at[:, there], back_own.at[q])

    def chunk(q, _):
        lanes = pl.ds(pl.multiple_of(q * CHUNK, 128), CHUNK)

        def levels(sg, _):
            for w in range(WIDE):
                for k in range(4):
                    tile[k * SLAB:(k + 1) * SLAB, w * CHUNK:(w + 1) * CHUNK] = stage[
                        k, q, pl.ds(sg * WIDE + w, SLAB, stride=STACK), :]

            def turn(t, _):
                w_t = wt[t, :, lanes].astype(F32)
                w_t = jnp.concatenate([w_t] * WIDE, 1)
                x = tile[...]
                tile[...] = x + increment(x, left[t], change[t], w_t)
                return 0

            lax.fori_loop(0, TURNS, turn, 0)
            for w in range(WIDE):
                for k in range(4):
                    outbox[k, q, pl.ds(sg * WIDE + w, SLAB, stride=STACK), :] = tile[
                        k * SLAB:(k + 1) * SLAB, w * CHUNK:(w + 1) * CHUNK]
            return 0

        lax.fori_loop(0, STACK // WIDE, levels, 0)
        for copy in send_back(q):
            copy.start()
        return 0

    lax.fori_loop(0, CHUNKS, chunk, 0)
    for q in range(CHUNKS):
        for copy in send_back(q):
            copy.wait()


def body(ensemble, loc_weight, obs_value, obs_var, owner_region, obs_cell, batch_order):
    flat = ensemble.reshape(SLAB * STACK, COLS_REG)
    smem, vmem, anywhere = (pl.BlockSpec(memory_space=m) for m in (pltpu.SMEM, pltpu.VMEM, pl.ANY))
    picked = pl.pallas_call(
        pick_kernel,
        out_shape=jax.ShapeDtypeStruct((TURNS, 24, OBS), F32),
        in_specs=[smem, smem, vmem, anywhere],
        out_specs=vmem,
        scratch_shapes=[pltpu.VMEM((SLAB * STACK, COLS_REG), F32), pltpu.SemaphoreType.DMA],
        compiler_params=pltpu.CompilerParams(vmem_limit_bytes=48 << 20),
        name="pick",
    )(batch_order, owner_region, obs_cell, flat)

    qa, qd = A_ROWS // 24, D_ROWS // 24
    dma = pltpu.SemaphoreType.DMA
    out = pl.pallas_call(
        main_kernel,
        out_shape=jax.ShapeDtypeStruct((SLAB * STACK, COLS_REG), F32),
        in_specs=[smem, smem, vmem, vmem, vmem, vmem, vmem, anywhere],
        out_specs=anywhere,
        scratch_shapes=[
            pltpu.VMEM((4, CHUNKS, SLAB * STACK, CHUNK), F32),
            pltpu.VMEM((4, CHUNKS, SLAB * STACK, CHUNK), F32),
            pltpu.VMEM((A_ROWS, OBS), F32), pltpu.VMEM((A_ROWS, OBS), F32),
            pltpu.VMEM((D_ROWS, OBS), F32), pltpu.VMEM((D_ROWS, OBS), F32),
            pltpu.VMEM((TURNS, OBS, COLS_DEV), BF16),
            pltpu.VMEM((len(CROSS), OBS, OBS), BF16),
            pltpu.VMEM((TURNS, MEM, OBS), F32),
            pltpu.VMEM((TURNS, OBS, 3 * MEM), BF16),
            pltpu.VMEM((TURNS, 2 * MEM, OBS), BF16),
            pltpu.VMEM((MEM, WIDE * CHUNK), F32),
            pltpu.VMEM((12 * qa, OBS), F32), pltpu.VMEM((3, 3, 3, qa, OBS), F32),
            pltpu.VMEM((12 * qd, OBS), F32), pltpu.VMEM((3, 3, 3, qd, OBS), F32),
            dma((CHUNKS, 3)), dma((CHUNKS, 3)), dma((CHUNKS,)),
            dma((CHUNKS, 3)), dma((CHUNKS, 3)), dma((CHUNKS,)),
            dma((4,)), dma((4, 3, 3)), dma((4, 3, 3)),
            dma((4,)), dma((4, 3, 3)), dma((4, 3, 3)),
        ],
        compiler_params=pltpu.CompilerParams(
            collective_id=0, has_side_effects=True, vmem_limit_bytes=56 << 20),
        name="filter",
    )(batch_order, owner_region, obs_cell, obs_value, obs_var, loc_weight, picked, flat)
    return out.reshape(SLAB, STACK, COLS_REG)


def solution(mesh):
    return jax.shard_map(
        body,
        mesh=mesh,
        in_specs=(P("grp", None, "region"), P(None, ("region", "grp"), None), P(), P(), P(), P(), P()),
        out_specs=P("grp", None, "region"),
        check_vma=False,
    )
```

time: 1540 us -> 183 us (0.12)
  waiting for transfers between devices: 1100 us -> 0 us
  Pallas kernels: 0 us -> 175 us
  matrix products: 137 us -> 0 us
  local copies, waits for them, and re-layouts: 135 us -> 7.95 us
  other arithmetic: 62.7 us -> 0 us
  between operations: 39.6 us -> 0.03 us
  blocking collectives: 35.7 us -> 0 us
  starting transfers between devices: 15.4 us -> 0 us
    psum x16 -> x0, waiting for transfers between devices: 1100 us -> none  [the longest x8 798 us: spread_2(): return lax.psum(kept, axis)]
    pallas_call x0 -> x2, Pallas kernels: none -> 175 us  [the longest x1 174 us: body(): pl.pallas_call(main_kernel, out_shape=jax.ShapeDtypeStruct((SLAB * STACK,...]
    dot_general x16 -> x0, matrix products: 137 us -> none  [the longest x8 71.9 us: regress(): lax.dot_general(change, kalman_gain, (((1,), (1,)), ((), ())), precision=...]
    unnamed x61 -> x11, local copies, waits for them, and re-layouts: 63.1 us -> 7.95 us
    all_to_all x1 -> x0, blocking collectives: 35.7 us -> none  [body(): return lax.all_to_all(state, 'grp', split_axis=0, concat_axis=2, tiled=True)]
    reshape x8 -> x0, local copies, waits for them, and re-layouts: 31.3 us -> none  [body(): state.reshape(members, stack * cols_dev)]
    reduce_sum x33 -> x0, other arithmetic: 29.6 us -> none  [the longest x16 14.6 us: statistics(): spread = jnp.sum(obs_anom * obs_anom, 0) / (members - 1) + epsilon]
    gather x16 -> x0, local copies, waits for them, and re-layouts: 23.9 us -> none  [body(): jnp.take(state.reshape(members, stack * cols_dev), flat_idx, axis=1)]
  transfers between devices with their start and end apart: 17 -> 0, of which waited for: 17 -> 0; matrix products, arithmetic and copies ran while one was open for 0% -> 0% of each run, Pallas kernels for 0% -> 0%
where the time goes in v1:
time: 183 us
  Pallas kernels  175 us (96%)
  local copies, waits for them, and re-layouts  7.95 us (4%)
    pallas_call x1, Pallas kernels, body(): pl.pallas_call(main_kernel, out_shape=jax.ShapeDtypeStruct((SLAB * STACK,...  174 us
    unnamed x11, local copies, waits for them, and re-layouts  7.95 us

profile of v1, /device:TPU:1, one launch (start us, length us, event | category | flops | bytes accessed | tf_op | source)
XLA Modules:
  0.0 183.0 jit_solution(18191971962462940895)
XLA Ops:
  0.0 0.0 copy-start
  0.0 1.7 copy-done
  1.7 0.0 copy-start.2
  1.7 0.7 copy-done.2
  2.4 0.0 copy-start.3
  2.4 0.7 copy-done.3
  3.1 0.0 copy-start.4
  3.1 0.7 copy-done.4
  3.8 0.8 pick.1.picked
  4.5 0.0 copy-start.1
  4.6 0.7 copy-done.1
  5.2 174.3 %filter.1 = f32[320,2048]{1,0:T(8,128)} custom-call(s32[8]{0:T(128)} %order.3, s32[8]{0:T(128)} %owner.3, s32[8,256]{1,0:T(8,128)} %cells.3, f32[8,256]{1,0:T(8,128)} %values.1, f32[8,256]{1,0:T(8,128)} %variances.1, bf16[8,512,256]{2,1,0:T(8,128)(2,1)} %weights.1, f32[8,24,256]{2,1,0:T(8,128)} %copy-done.1, f32[320,2048]{1,0:T(8,128)} %bitcast.2), custom_call_target="tpu_custom_call" | custom-call | tf_op jit(solution)/shard_map/filter/pallas_call | solution.py:299
  179.5 3.5 %copy.9 = f32[20,16,2048]{2,1,0:T(8,128)} copy(f32[20,16,2048]{2,1,0:T(8,128)} %bitcast.4) | data formatting | bytes 5242880
Async XLA Ops:
  0.0 1.7 copy-start
  1.7 0.7 copy-start.2
  2.4 0.7 copy-start.3
  3.1 0.7 copy-start.4
  4.5 0.7 copy-start.1

commit v2 on v1

v2 whole, which is shorter than its diff:
```python
import functools

import jax
import jax.numpy as jnp
from jax import lax
from jax.experimental import pallas as pl
from jax.experimental.pallas import tpu as pltpu
from jax.sharding import PartitionSpec as P

epsilon = 1e-05
MESH = pl.DeviceIdType.MESH
F32, BF16 = jnp.float32, jnp.bfloat16

TURNS, OBS, MEM, SLAB, STACK = 8, 256, 80, 20, 16
COLS_REG, COLS_DEV = 2048, 512
GROUP = 4
FIRST = [(a, b) for b in range(GROUP) for a in range(b)]
SECOND = [(a, b) for b in range(GROUP, TURNS) for a in range(GROUP, b)]
CROSS = [(a, b) for b in range(GROUP, TURNS) for a in range(GROUP)]
FIRST_ROW = {p: i * OBS for i, p in enumerate(FIRST)}
SECOND_ROW = {p: i * OBS for i, p in enumerate(SECOND)}
CROSS_AT = {p: i for i, p in enumerate(CROSS)}
X0_ROW = len(FIRST) * OBS
A_ROWS = 2560
B_ROWS = len(SECOND) * OBS
D_ROWS = 384
CHUNKS, CHUNK = 4, 128
CELLS = STACK * CHUNK


def split2(value):
    high = value.astype(BF16)
    low = (value - high.astype(F32)).astype(BF16)
    return high, low


def increment(x, left, change, weights):
    anom = x - jnp.sum(x, 0, keepdims=True) * (1.0 / MEM)
    high, low = split2(anom)
    stacked = jnp.concatenate([high, high, low], 0)
    gain = jnp.dot(left, stacked, preferred_element_type=F32) * weights
    g_high, g_low = split2(gain)
    first = jnp.dot(change, g_high, preferred_element_type=F32)
    second = jnp.dot(change[:MEM], g_low, preferred_element_type=F32)
    return first[:MEM] + first[MEM:] + second


def turn_operands(prior, value, variance):
    centre = jnp.sum(prior, 0, keepdims=True) * (1.0 / MEM)
    anom = prior - centre
    spread = jnp.sum(anom * anom, 0, keepdims=True) / (MEM - 1) + epsilon
    denom = spread + variance
    post = (variance * centre + spread * value) / denom
    factor = jnp.sqrt(variance / denom)
    change = post + factor * anom - prior
    scaled = anom * (1.0 / ((MEM - 1) * spread))
    high = scaled.astype(BF16).astype(F32)
    low = scaled - high
    left = jnp.concatenate([high, low, high], 0).T.astype(BF16)
    c_high, c_low = split2(change)
    return left, jnp.concatenate([c_high, c_low], 0)


def pick_kernel(order, owner, cells, ens, out, held, sem):
    here = lax.axis_index("region")
    out[...] = jnp.zeros_like(out)
    mine = [owner[order[t]] == here for t in range(TURNS)]
    some = functools.reduce(jnp.logical_or, mine)

    @pl.when(some)
    def _():
        copy = pltpu.make_async_copy(ens, held, sem)
        copy.start()
        copy.wait()

    for t in range(TURNS):

        @pl.when(mine[t])
        def _(t=t):
            cell = cells[pl.ds(order[t], 1), :]
            column = cell & (COLS_REG - 1)
            level = cell >> 11
            depth = 512

            def part(k, total):
                at = pl.multiple_of(k * depth, depth)
                rows = lax.broadcasted_iota(jnp.int32, (depth, OBS), 0) + at
                select = jnp.where(rows == column, 1.0, 0.0).astype(BF16)
                value = held[:, pl.ds(at, depth)]
                high = value.astype(BF16)
                rest = value - high.astype(F32)
                middle, low = split2(rest)
                for piece in (high, middle, low):
                    total = total + jnp.dot(piece, select, preferred_element_type=F32)
                return total

            total = lax.fori_loop(0, COLS_REG // depth, part, jnp.zeros((SLAB * STACK, OBS), F32))
            total = total.reshape(SLAB, STACK, OBS)
            levels = lax.broadcasted_iota(jnp.int32, (SLAB, STACK, OBS), 1)
            out[t, 0:SLAB, :] = jnp.sum(jnp.where(levels == level[None], total, 0.0), 1)


def places():
    region, z = lax.axis_index("region"), lax.axis_index("grp")
    return region // 8, (region // 2) % 4, region % 2, z


def peer(axis, k):
    x, y, c, z = places()
    if axis == "x":
        x = lax.rem(x + k, 4)
    elif axis == "y":
        y = lax.rem(y + k, 4)
    elif axis == "z":
        z = lax.rem(z + k, 4)
    else:
        c = 1 - c
    return (x * 8 + y * 2 + c, z)


def remote(src, dst, send, recv, device):
    return pltpu.make_async_remote_copy(src, dst, send, recv, device_id=device, device_id_type=MESH)


def started(copies):
    for copy in copies:
        copy.start()
    return copies


def wait(copies):
    for copy in copies:
        copy.wait()


def swap_halves(src, dst, sems, k):
    return started([remote(src, dst, sems.at[2 * k], sems.at[2 * k + 1], peer("c", 1))])


def small_sum(a, b, rows, sib, inbox, sib_sem, send, recv):
    x, y, c, z = places()
    at = {"x": x, "y": y, "z": z}
    axes = ("x", "y", "z")
    q = rows // 24
    t, h = 4 * q, 12 * q
    base, other = pl.multiple_of(c * h, 8), pl.multiple_of((1 - c) * h, 8)
    own = [pl.multiple_of(base + i * t + at[axes[i]] * q, 8) for i in range(3)]

    copies = swap_halves(a.at[pl.ds(other, h)], sib, sib_sem, 0)
    yield
    wait(copies)
    a[pl.ds(base, h), :] += sib[...]
    for phase in range(3):
        copies = []
        for k in (1, 2, 3):
            for i in range(3):
                axis = axes[(i + phase) % 3]
                src = own[i]
                if phase == 0:
                    src = pl.multiple_of(base + i * t + lax.rem(at[axis] + k, 4) * q, 8)
                copies.append(remote(a.at[pl.ds(src, q)], inbox.at[phase, i, k - 1], send.at[phase, i, k - 1],
                                     recv.at[phase, i, k - 1], peer(axis, k)))
        started(copies)
        yield
        wait(copies)
        for i in range(3):
            into = b if phase == 2 else a
            into[pl.ds(own[i], q), :] = (
                a[pl.ds(own[i], q), :] + inbox[phase, i, 0] + inbox[phase, i, 1] + inbox[phase, i, 2])
    copies = []
    for k in (1, 2, 3):
        for i in range(3):
            rows_i = b.at[pl.ds(own[i], q)]
            copies.append(remote(rows_i, rows_i, send.at[3, i, k - 1], recv.at[3, i, k - 1], peer(axes[i], k)))
    started(copies)
    yield
    wait(copies)
    half = b.at[pl.ds(base, h)]
    copies = swap_halves(half, half, sib_sem, 1)
    yield
    wait(copies)


def big_sum(a, b, rows, sib, in0, in1, in2, sib_sem, send, recv):
    x, y, c, z = places()
    at = {"x": x, "y": y}
    orders = (("x", "y"), ("y", "x"))
    h = rows // 2
    t = h // 2
    q, r = t // 4, t // 16
    base, other = pl.multiple_of(c * h, 8), pl.multiple_of((1 - c) * h, 8)
    block = [pl.multiple_of(base + i * t, 8) for i in range(2)]
    quarter = [pl.multiple_of(block[i] + at[orders[i][0]] * q, 8) for i in range(2)]
    own = [pl.multiple_of(quarter[i] + at[orders[i][1]] * r, 8) for i in range(2)]

    copies = swap_halves(a.at[pl.ds(other, h)], sib, sib_sem, 0)
    yield
    wait(copies)
    a[pl.ds(base, h), :] += sib[...]

    def exchange(phase, pick, inbox, axis_of):
        return started([
            remote(a.at[pl.ds(pick(i, k), inbox.shape[2])], inbox.at[i, k - 1], send.at[phase, i, k - 1],
                   recv.at[phase, i, k - 1], peer(axis_of(i), k))
            for k in (1, 2, 3) for i in range(2)])

    def added(i, at, inbox):
        return a[pl.ds(at, inbox.shape[2]), :] + inbox[i, 0] + inbox[i, 1] + inbox[i, 2]

    copies = exchange(0, lambda i, k: pl.multiple_of(block[i] + lax.rem(at[orders[i][0]] + k, 4) * q, 8),
                      in0, lambda i: orders[i][0])
    yield
    wait(copies)
    for i in range(2):
        a[pl.ds(quarter[i], q), :] = added(i, quarter[i], in0)
    copies = exchange(1, lambda i, k: pl.multiple_of(quarter[i] + lax.rem(at[orders[i][1]] + k, 4) * r, 8),
                      in1, lambda i: orders[i][1])
    yield
    wait(copies)
    for i in range(2):
        a[pl.ds(own[i], r), :] = added(i, own[i], in1)
    copies = exchange(2, lambda i, k: own[i], in2, lambda i: "z")
    yield
    wait(copies)
    for i in range(2):
        b[pl.ds(own[i], r), :] = added(i, own[i], in2)

    def gather(phase, place, size, axis_of):
        return started([
            remote(b.at[pl.ds(place[i], size)], b.at[pl.ds(place[i], size)], send.at[phase, i, k - 1],
                   recv.at[phase, i, k - 1], peer(axis_of(i), k))
            for k in (1, 2, 3) for i in range(2)])

    copies = gather(3, own, r, lambda i: orders[i][1])
    yield
    wait(copies)
    copies = gather(4, quarter, q, lambda i: orders[i][0])
    yield
    wait(copies)
    half = b.at[pl.ds(base, h)]
    copies = swap_halves(half, half, sib_sem, 1)
    yield
    wait(copies)


def main_kernel(order, owner, cells, values, variances, weights, picked, ens, out,
                stage, outbox, state, wt, cross, prior, left, change,
                a, a_sum, b, b_sum, d, d_sum, *rest):
    (sib_a, in0_a, in1_a, in2_a, sib_b, in0_b, in1_b, in2_b, sib_d, in_d,
     go_send, go_recv, go_own, back_send, back_recv, back_own,
     sibsem_a, send_a, recv_a, sibsem_b, send_b, recv_b, sibsem_d, send_d, recv_d) = rest
    region, z = lax.axis_index("region"), lax.axis_index("grp")

    barrier = pltpu.get_barrier_semaphore()
    around = [peer(axis, k) for axis in ("x", "y", "z") for k in (1, 2, 3)] + [peer("c", 1)]
    for device in around:
        pl.semaphore_signal(barrier, 1, device_id=device, device_id_type=MESH)
    pl.semaphore_wait(barrier, len(around))

    def go(q):
        here = pl.ds(pl.multiple_of(z * COLS_DEV + q * CHUNK, 128), CHUNK)
        copies = [pltpu.make_async_copy(ens.at[:, here], stage.at[z, q], go_own.at[q])]
        for k in (1, 2, 3):
            there = pl.ds(pl.multiple_of(lax.rem(z + k, 4) * COLS_DEV + q * CHUNK, 128), CHUNK)
            copies.append(remote(ens.at[:, there], stage.at[z, q], go_send.at[q, k - 1], go_recv.at[q, k - 1],
                                 peer("z", k)))
        return started(copies)

    def back(q):
        there = pl.ds(pl.multiple_of(z * COLS_DEV + q * CHUNK, 128), CHUNK)
        copies = [pltpu.make_async_copy(outbox.at[z, q], out.at[:, there], back_own.at[q])]
        for k in (1, 2, 3):
            copies.append(remote(outbox.at[lax.rem(z + k, 4), q], out.at[:, there],
                                 back_send.at[q, k - 1], back_recv.at[q, k - 1], peer("z", k)))
        return copies

    def turned(t):
        wt[t] = weights[order[t]].astype(F32).T.astype(BF16)

    def select(n):
        column = cells[pl.ds(order[n], 1), :] & (COLS_REG - 1)
        local = jnp.where(owner[order[n]] == region, column - z * COLS_DEV, -1)
        return jnp.where(lax.broadcasted_iota(jnp.int32, (COLS_DEV, OBS), 0) == local, 1.0, 0.0).astype(BF16)

    def at_columns(t, chosen):
        return jnp.dot(wt[t], chosen, preferred_element_type=F32)

    sent = go(0) + go(1)
    for t in range(GROUP - 1):
        turned(t)
    for n in range(TURNS):
        if 0 < n < GROUP:
            chosen = select(n)
            for t in range(n):
                row = FIRST_ROW[t, n]
                a[row:row + OBS, :] = at_columns(t, chosen)
        for k in range(4):
            at = X0_ROW + n * MEM + k * SLAB
            a[at:at + SLAB, :] = jnp.where(z == k, picked[n, 0:SLAB, :], 0.0)
    a[X0_ROW + TURNS * MEM:A_ROWS, :] = jnp.zeros((A_ROWS - X0_ROW - TURNS * MEM, OBS), F32)

    sum_a = big_sum(a, a_sum, A_ROWS, sib_a, in0_a, in1_a, in2_a, sibsem_a, send_a, recv_a)
    sum_b = big_sum(b, b_sum, B_ROWS, sib_b, in0_b, in1_b, in2_b, sibsem_b, send_b, recv_b)
    sum_d = small_sum(d, d_sum, D_ROWS, sib_d, in_d, sibsem_d, send_d, recv_d)

    next(sum_a)
    for t in range(GROUP - 1, TURNS):
        turned(t)
    next(sum_a)
    for n in range(GROUP, TURNS):
        chosen = select(n)
        for t in range(n):
            rows = at_columns(t, chosen)
            if t < GROUP:
                cross[CROSS_AT[t, n]] = rows.astype(BF16)
            else:
                row = SECOND_ROW[t, n]
                b[row:row + OBS, :] = rows
    d[...] = jnp.zeros_like(d)
    next(sum_b)
    next(sum_a)
    next(sum_a)
    next(sum_b)
    next(sum_a)
    next(sum_b)
    sent += go(2) + go(3)
    next(sum_a)
    next(sum_b)
    next(sum_a)
    next(sum_a, None)

    def assimilate(t):
        left[t], change[t] = turn_operands(
            prior[t], values[pl.ds(order[t], 1), :], variances[pl.ds(order[t], 1), :])

    for n in range(TURNS):
        prior[n] = a_sum[X0_ROW + n * MEM:X0_ROW + (n + 1) * MEM, :]
    for t in range(GROUP):
        assimilate(t)
        for n in range(t + 1, TURNS):
            if n < GROUP:
                row = FIRST_ROW[t, n]
                prior[n] += increment(prior[n], left[t], change[t], a_sum[row:row + OBS, :])
            else:
                at = (n - GROUP) * MEM
                step = increment(prior[n], left[t], change[t], cross[CROSS_AT[t, n]].astype(F32))
                d[at:at + MEM, :] += step
                prior[n] += step
    next(sum_d)
    next(sum_b)

    def turns(q, first, last):
        lanes = pl.ds(pl.multiple_of(q * CHUNK, 128), CHUNK)

        def turn(t, _):
            w_t = jnp.concatenate([wt[t, :, lanes].astype(F32)] * STACK, 1)
            x = state[q]
            state[q] = x + increment(x, left[t], change[t], w_t)
            return 0

        lax.fori_loop(first, last, turn, 0)

    def early(q):
        def level(s, _):
            lanes = pl.ds(pl.multiple_of(s * CHUNK, 128), CHUNK)
            for k in range(4):
                state[q, k * SLAB:(k + 1) * SLAB, lanes] = stage[k, q, pl.ds(s, SLAB, stride=STACK), :]
            return 0

        lax.fori_loop(0, STACK, level, 0)
        turns(q, 0, GROUP)

    next(sum_d)
    wait(sent)
    early(0)
    next(sum_d)
    next(sum_b)
    early(1)
    next(sum_d)
    next(sum_b)
    early(2)
    next(sum_d)
    next(sum_b, None)
    early(3)
    next(sum_d)
    next(sum_d, None)

    for n in range(GROUP, TURNS):
        at = (n - GROUP) * MEM
        prior[n] = a_sum[X0_ROW + n * MEM:X0_ROW + (n + 1) * MEM, :] + d_sum[at:at + MEM, :]
    for t in range(GROUP, TURNS):
        assimilate(t)
        for n in range(t + 1, TURNS):
            row = SECOND_ROW[t, n]
            prior[n] += increment(prior[n], left[t], change[t], b_sum[row:row + OBS, :])

    def late(q, _):
        turns(q, GROUP, TURNS)

        def level(s, _):
            lanes = pl.ds(pl.multiple_of(s * CHUNK, 128), CHUNK)
            for k in range(4):
                outbox[k, q, pl.ds(s, SLAB, stride=STACK), :] = state[q, k * SLAB:(k + 1) * SLAB, lanes]
            return 0

        lax.fori_loop(0, STACK, level, 0)
        started(back(q))
        return 0

    lax.fori_loop(0, CHUNKS, late, 0)
    for q in range(CHUNKS):
        wait(back(q))


def body(ensemble, loc_weight, obs_value, obs_var, owner_region, obs_cell, batch_order):
    flat = ensemble.reshape(SLAB * STACK, COLS_REG)
    smem, vmem, anywhere = (pl.BlockSpec(memory_space=m) for m in (pltpu.SMEM, pltpu.VMEM, pl.ANY))
    picked = pl.pallas_call(
        pick_kernel,
        out_shape=jax.ShapeDtypeStruct((TURNS, 24, OBS), F32),
        in_specs=[smem, smem, vmem, anywhere],
        out_specs=vmem,
        scratch_shapes=[pltpu.VMEM((SLAB * STACK, COLS_REG), F32), pltpu.SemaphoreType.DMA],
        compiler_params=pltpu.CompilerParams(vmem_limit_bytes=60 << 20),
        name="pick",
    )(batch_order, owner_region, obs_cell, flat)

    dma = pltpu.SemaphoreType.DMA

    def big_room(rows):
        return [pltpu.VMEM((rows // 2, OBS), F32)] + [
            pltpu.VMEM((2, 3, rows // cut, OBS), F32) for cut in (16, 64, 64)]

    out = pl.pallas_call(
        main_kernel,
        out_shape=jax.ShapeDtypeStruct((SLAB * STACK, COLS_REG), F32),
        in_specs=[smem, smem, vmem, vmem, vmem, vmem, vmem, anywhere],
        out_specs=anywhere,
        scratch_shapes=[
            pltpu.VMEM((4, CHUNKS, SLAB * STACK, CHUNK), F32),
            pltpu.VMEM((4, CHUNKS, SLAB * STACK, CHUNK), F32),
            pltpu.VMEM((CHUNKS, MEM, CELLS), F32),
            pltpu.VMEM((TURNS, OBS, COLS_DEV), BF16),
            pltpu.VMEM((len(CROSS), OBS, OBS), BF16),
            pltpu.VMEM((TURNS, MEM, OBS), F32),
            pltpu.VMEM((TURNS, OBS, 3 * MEM), BF16),
            pltpu.VMEM((TURNS, 2 * MEM, OBS), BF16),
            pltpu.VMEM((A_ROWS, OBS), F32), pltpu.VMEM((A_ROWS, OBS), F32),
            pltpu.VMEM((B_ROWS, OBS), F32), pltpu.VMEM((B_ROWS, OBS), F32),
            pltpu.VMEM((D_ROWS, OBS), F32), pltpu.VMEM((D_ROWS, OBS), F32),
            *big_room(A_ROWS), *big_room(B_ROWS),
            pltpu.VMEM((D_ROWS // 2, OBS), F32), pltpu.VMEM((3, 3, 3, D_ROWS // 24, OBS), F32),
            dma((CHUNKS, 3)), dma((CHUNKS, 3)), dma((CHUNKS,)),
            dma((CHUNKS, 3)), dma((CHUNKS, 3)), dma((CHUNKS,)),
            dma((4,)), dma((5, 2, 3)), dma((5, 2, 3)),
            dma((4,)), dma((5, 2, 3)), dma((5, 2, 3)),
            dma((4,)), dma((4, 3, 3)), dma((4, 3, 3)),
        ],
        compiler_params=pltpu.CompilerParams(
            collective_id=0, has_side_effects=True, vmem_limit_bytes=60 << 20),
        name="filter",
    )(batch_order, owner_region, obs_cell, obs_value, obs_var, loc_weight, picked, flat)
    return out.reshape(SLAB, STACK, COLS_REG)


def solution(mesh):
    return jax.shard_map(
        body,
        mesh=mesh,
        in_specs=(P("grp", None, "region"), P(None, ("region", "grp"), None), P(), P(), P(), P(), P()),
        out_specs=P("grp", None, "region"),
        check_vma=False,
    )
```

time: 183 us -> 119 us (0.65)
  Pallas kernels: 175 us -> 115 us
  local copies, waits for them, and re-layouts: 7.95 us -> 3.53 us
    pallas_call x1, Pallas kernels: 174 us -> 114 us  [body(): pl.pallas_call(main_kernel, out_shape=jax.ShapeDtypeStruct((SLAB * STACK,...]
    unnamed x11 -> x1, local copies, waits for them, and re-layouts: 7.95 us -> 3.53 us
where the time goes in v2:
time: 119 us
  Pallas kernels  115 us (97%)
  local copies, waits for them, and re-layouts  3.53 us (3%)
    pallas_call x1, Pallas kernels, body(): pl.pallas_call(main_kernel, out_shape=jax.ShapeDtypeStruct((SLAB * STACK,...  114 us
    unnamed x1, local copies, waits for them, and re-layouts  3.53 us

profile of v2, /device:TPU:1, one launch (start us, length us, event | category | flops | bytes accessed | tf_op | source)
XLA Modules:
  0.0 118.8 jit_solution(8887048879834267012)
XLA Ops:
  0.0 1.4 %pick.1.picked = f32[8,24,256]{2,1,0:T(8,128)} custom-call(s32[8]{0:T(128)} %order.3, s32[8]{0:T(128)} %owner.3, s32[8,256]{1,0:T(8,128)} %cells.3, f32[320,2048]{1,0:T(8,128)} %bitcast.2), custom_call_target="tpu_custom_call" | custom-call | tf_op jit(solution)/shard_map/pick/pallas_call | solution.py:418
  1.5 113.8 %filter.1 = f32[320,2048]{1,0:T(8,128)} custom-call(s32[8]{0:T(128)} %order.3, s32[8]{0:T(128)} %owner.3, s32[8,256]{1,0:T(8,128)} %cells.3, f32[8,256]{1,0:T(8,128)} %values.1, f32[8,256]{1,0:T(8,128)} %variances.1, bf16[8,512,256]{2,1,0:T(8,128)(2,1)} %weights.1, f32[8,24,256]{2,1,0:T(8,128)} %pick.1.picked, f32[320,2048]{1,0:T(8,128)} %bitcast.3), custom_call_target="tpu_custom_call" | custom-call | tf_op jit(solution)/shard_map/filter/pallas_call | solution.py:434
  115.3 3.5 %copy.9 = f32[20,16,2048]{2,1,0:T(8,128)} copy(f32[20,16,2048]{2,1,0:T(8,128)} %bitcast.4) | data formatting | bytes 5242880

commit v3 on v2

v3 whole, which is shorter than its diff:
```python
import functools

import jax
import jax.numpy as jnp
from jax import lax
from jax.experimental import pallas as pl
from jax.experimental.pallas import tpu as pltpu
from jax.sharding import PartitionSpec as P

epsilon = 1e-05
MESH = pl.DeviceIdType.MESH
F32, BF16 = jnp.float32, jnp.bfloat16

TURNS, OBS, MEM, SLAB, STACK = 8, 256, 80, 20, 16
COLS_REG, COLS_DEV = 2048, 512
GROUP = 4
LANES = 128
FIRST = [(a, b) for b in range(GROUP) for a in range(b)]
SECOND = [(a, b) for b in range(GROUP, TURNS) for a in range(GROUP, b)]
CROSS = [(a, b) for b in range(GROUP, TURNS) for a in range(GROUP)]
FIRST_ROW = {p: i * OBS for i, p in enumerate(FIRST)}
SECOND_ROW = {p: i * OBS for i, p in enumerate(SECOND)}
CROSS_AT = {p: i for i, p in enumerate(CROSS)}
A_ROWS = 2 * len(FIRST) * OBS
B_ROWS = 2 * len(SECOND) * OBS
D_USED = 2 * (TURNS - GROUP) * MEM
D_ROWS = -(-D_USED // 128) * 128
X_ROWS = TURNS * 24 // 2
CHUNKS, CHUNK = 4, 128
CELLS = STACK * CHUNK
EARLY = [GROUP, GROUP - 1, GROUP - 1, GROUP - 1]


def split2(value):
    high = value.astype(BF16)
    low = (value - high.astype(F32)).astype(BF16)
    return high, low


def increment(x, left, change, weights):
    anom = x - jnp.sum(x, 0, keepdims=True) * (1.0 / MEM)
    high, low = split2(anom)
    stacked = jnp.concatenate([high, high, low], 0)
    gain = jnp.dot(left, stacked, preferred_element_type=F32) * weights
    g_high, g_low = split2(gain)
    first = jnp.dot(change, g_high, preferred_element_type=F32)
    second = jnp.dot(change[:MEM], g_low, preferred_element_type=F32)
    return first[:MEM] + first[MEM:] + second


def turn_operands(prior, value, variance):
    centre = jnp.sum(prior, 0, keepdims=True) * (1.0 / MEM)
    anom = prior - centre
    spread = jnp.sum(anom * anom, 0, keepdims=True) / (MEM - 1) + epsilon
    denom = spread + variance
    post = (variance * centre + spread * value) / denom
    factor = jnp.sqrt(variance / denom)
    change = post + factor * anom - prior
    scaled = anom * (1.0 / ((MEM - 1) * spread))
    high = scaled.astype(BF16).astype(F32)
    low = scaled - high
    left = jnp.concatenate([high, low, high], 0).T.astype(BF16)
    c_high, c_low = split2(change)
    return left, jnp.concatenate([c_high, c_low], 0)


def pick_kernel(order, owner, cells, ens, out, held, pieces, total, sems):
    here = lax.axis_index("region")
    depth = COLS_REG // 4
    out[...] = jnp.zeros_like(out)
    some = functools.reduce(jnp.logical_or, [owner[order[t]] == here for t in range(TURNS)])

    def columns_of(k):
        return pl.ds(pl.multiple_of(k * depth, depth), depth)

    def fetch(k):
        return pltpu.make_async_copy(ens.at[:, columns_of(k)], held.at[k], sems.at[k])

    def cell_of(t):
        return cells[pl.ds(order[t], 1), :]

    @pl.when(some)
    def _():
        for k in range(4):
            fetch(k).start()

        def part(k, _):
            fetch(k).wait()
            value = held[k]
            high = value.astype(BF16)
            middle, low = split2(value - high.astype(F32))
            pieces[...] = jnp.concatenate([high, middle, low], 0)

            def batch(t, _):
                @pl.when(owner[order[t]] == here)
                def _():
                    column = cell_of(t) & (COLS_REG - 1)
                    rows = lax.broadcasted_iota(jnp.int32, (depth, OBS), 0) + k * depth
                    select = jnp.where(rows == column, 1.0, 0.0).astype(BF16)
                    got = jnp.dot(pieces[...], select, preferred_element_type=F32)
                    n = SLAB * STACK
                    got = got[:n] + got[n:2 * n] + got[2 * n:]
                    total[t] = jnp.where(k == 0, got, total[t] + got)

                return 0

            lax.fori_loop(0, TURNS, batch, 0)
            return 0

        lax.fori_loop(0, 4, part, 0)

        def finish(t, _):
            @pl.when(owner[order[t]] == here)
            def _():
                levels = lax.broadcasted_iota(jnp.int32, (SLAB, STACK, OBS), 1)
                values = total[t].reshape(SLAB, STACK, OBS)
                level = (cell_of(t) >> 11)[None]
                out[t, 0:SLAB, :] = jnp.sum(jnp.where(levels == level, values, 0.0), 1)

            return 0

        lax.fori_loop(0, TURNS, finish, 0)


def places():
    region, z = lax.axis_index("region"), lax.axis_index("grp")
    return region // 8, (region // 2) % 4, region % 2, z


def peer(axis, k):
    x, y, c, z = places()
    if axis == "x":
        x = lax.rem(x + k, 4)
    elif axis == "y":
        y = lax.rem(y + k, 4)
    elif axis == "z":
        z = lax.rem(z + k, 4)
    else:
        c = 1 - c
    return (x * 8 + y * 2 + c, z)


def remote(src, dst, send, recv, device):
    return pltpu.make_async_remote_copy(src, dst, send, recv, device_id=device, device_id_type=MESH)


def started(copies):
    for copy in copies:
        copy.start()
    return copies


def wait(copies):
    for copy in copies:
        copy.wait()


def swap_halves(src, dst, sems, k):
    return started([remote(src, dst, sems.at[2 * k], sems.at[2 * k + 1], peer("c", 1))])


def all_sum(a, b, rows, twice, sib, in0, in1, in2, sib_sem, send, recv):
    x, y, c, z = places()
    at = {"x": x, "y": y}
    orders = (("x", "y"), ("y", "x"))
    h = rows // 2
    t = h // 2
    q = t // 4
    r = q // 4 if twice else q
    base, other = pl.multiple_of(c * h, 8), pl.multiple_of((1 - c) * h, 8)
    block = [pl.multiple_of(base + i * t, 8) for i in range(2)]
    quarter = [pl.multiple_of(block[i] + at[orders[i][0]] * q, 8) for i in range(2)]
    own = quarter
    if twice:
        own = [pl.multiple_of(quarter[i] + at[orders[i][1]] * r, 8) for i in range(2)]

    copies = swap_halves(a.at[pl.ds(other, h)], sib, sib_sem, 0)
    yield
    wait(copies)
    a[pl.ds(base, h), :] += sib[...]

    def exchange(phase, pick, inbox, axis_of):
        return started([
            remote(a.at[pl.ds(pick(i, k), inbox.shape[2])], inbox.at[i, k - 1], send.at[phase, i, k - 1],
                   recv.at[phase, i, k - 1], peer(axis_of(i), k))
            for k in (1, 2, 3) for i in range(2)])

    def added(i, at, inbox):
        return a[pl.ds(at, inbox.shape[2]), :] + inbox[i, 0] + inbox[i, 1] + inbox[i, 2]

    copies = exchange(0, lambda i, k: pl.multiple_of(block[i] + lax.rem(at[orders[i][0]] + k, 4) * q, 8),
                      in0, lambda i: orders[i][0])
    yield
    wait(copies)
    for i in range(2):
        a[pl.ds(quarter[i], q), :] = added(i, quarter[i], in0)

    def second(i, k):
        if twice:
            return pl.multiple_of(quarter[i] + lax.rem(at[orders[i][1]] + k, 4) * r, 8)
        return quarter[i]

    copies = exchange(1, second, in1, lambda i: orders[i][1])
    yield
    wait(copies)
    for i in range(2):
        a[pl.ds(own[i], r), :] = added(i, own[i], in1)
    copies = exchange(2, lambda i, k: own[i], in2, lambda i: "z")
    yield
    wait(copies)
    for i in range(2):
        b[pl.ds(own[i], r), :] = added(i, own[i], in2)

    def gather(phase, place, size, axis_of):
        return started([
            remote(b.at[pl.ds(place[i], size)], b.at[pl.ds(place[i], size)], send.at[phase, i, k - 1],
                   recv.at[phase, i, k - 1], peer(axis_of(i), k))
            for k in (1, 2, 3) for i in range(2)])

    if twice:
        copies = gather(3, own, r, lambda i: orders[i][1])
        yield
        wait(copies)
    copies = gather(4, quarter, q, lambda i: orders[i][0])
    yield
    wait(copies)
    half = b.at[pl.ds(base, h)]
    copies = swap_halves(half, half, sib_sem, 1)
    yield
    wait(copies)


def prior_sum(mine, half, all_of, sib, in0, in1, sib_sem, send, recv):
    x, y, c, z = places()
    orders = (("x", "y"), ("y", "x"))
    t = X_ROWS // 2
    base, other = pl.multiple_of(c * X_ROWS, 8), pl.multiple_of((1 - c) * X_ROWS, 8)

    copies = swap_halves(mine.at[pl.ds(other, X_ROWS)], sib, sib_sem, 0)
    yield
    wait(copies)
    half[...] = mine[pl.ds(base, X_ROWS), :] + sib[...]
    for phase, inbox in enumerate((in0, in1)):
        copies = started([
            remote(half.at[i * t:(i + 1) * t], inbox.at[i, k - 1], send.at[phase, i, k - 1], recv.at[phase, i, k - 1],
                   peer(orders[i][phase], k))
            for k in (1, 2, 3) for i in range(2)])
        yield
        wait(copies)
        for i in range(2):
            value = half[i * t:(i + 1) * t, :] + inbox[i, 0] + inbox[i, 1] + inbox[i, 2]
            if phase == 0:
                half[i * t:(i + 1) * t, :] = value
            else:
                all_of[c, z, i * t:(i + 1) * t, :] = value
    spot = all_of.at[c, z]
    copies = started([remote(spot, spot, send.at[2, 0, k - 1], recv.at[2, 0, k - 1], peer("z", k)) for k in (1, 2, 3)])
    yield
    wait(copies)
    spot = all_of.at[c]
    copies = swap_halves(spot, spot, sib_sem, 1)
    yield
    wait(copies)


def main_kernel(order, owner, cells, values, variances, weights, picked, ens, out,
                stage, outbox, state, wt, cross, prior, left, change,
                a, a_sum, b, b_sum, d, d_sum, *rest):
    (sib_a, in0_a, in1_a, in2_a, sib_b, in0_b, in1_b, in2_b, sib_d, in0_d, in1_d, in2_d, x_half, x_all, sib_x, in0_x, in1_x,
     go_send, go_recv, go_own, back_send, back_recv, back_own,
     sibsem_a, send_a, recv_a, sibsem_b, send_b, recv_b, sibsem_d, send_d, recv_d,
     sibsem_x, send_x, recv_x) = rest
    region, z = lax.axis_index("region"), lax.axis_index("grp")

    barrier = pltpu.get_barrier_semaphore()
    around = [peer(axis, k) for axis in ("x", "y", "z") for k in (1, 2, 3)] + [peer("c", 1)]
    for device in around:
        pl.semaphore_signal(barrier, 1, device_id=device, device_id_type=MESH)

    def go(q):
        here = pl.ds(pl.multiple_of(z * COLS_DEV + q * CHUNK, 128), CHUNK)
        copies = [pltpu.make_async_copy(ens.at[:, here], stage.at[z, q], go_own.at[q])]
        for k in (1, 2, 3):
            there = pl.ds(pl.multiple_of(lax.rem(z + k, 4) * COLS_DEV + q * CHUNK, 128), CHUNK)
            copies.append(remote(ens.at[:, there], stage.at[z, q], go_send.at[q, k - 1], go_recv.at[q, k - 1],
                                 peer("z", k)))
        return started(copies)

    def back(q):
        there = pl.ds(pl.multiple_of(z * COLS_DEV + q * CHUNK, 128), CHUNK)
        copies = [pltpu.make_async_copy(outbox.at[z, q], out.at[:, there], back_own.at[q])]
        for k in (1, 2, 3):
            copies.append(remote(outbox.at[lax.rem(z + k, 4), q], out.at[:, there],
                                 back_send.at[q, k - 1], back_recv.at[q, k - 1], peer("z", k)))
        return copies

    def turned(t):
        wt[t] = weights[order[t]].astype(F32).T.astype(BF16)

    def select(n):
        column = cells[pl.ds(order[n], 1), :] & (COLS_REG - 1)
        local = jnp.where(owner[order[n]] == region, column - z * COLS_DEV, -1)
        return jnp.where(lax.broadcasted_iota(jnp.int32, (COLS_DEV, OBS), 0) == local, 1.0, 0.0).astype(BF16)

    def at_columns(t, chosen):
        return jnp.dot(wt[t], chosen, preferred_element_type=F32)

    def put_pair(buffer, rows, row, value):
        buffer[row:row + OBS, :] = value[:, :LANES]
        buffer[rows // 2 + row:rows // 2 + row + OBS, :] = value[:, LANES:]

    def get_pair(buffer, rows, row):
        return jnp.concatenate([buffer[row:row + OBS, :], buffer[rows // 2 + row:rows // 2 + row + OBS, :]], 1)

    for t in range(GROUP - 1):
        turned(t)
    for n in range(1, GROUP):
        chosen = select(n)
        for t in range(n):
            put_pair(a, A_ROWS, FIRST_ROW[t, n], at_columns(t, chosen))

    sum_x = prior_sum(picked, x_half, x_all, sib_x, in0_x, in1_x, sibsem_x, send_x, recv_x)
    sum_a = all_sum(a, a_sum, A_ROWS, True, sib_a, in0_a, in1_a, in2_a, sibsem_a, send_a, recv_a)
    sum_b = all_sum(b, b_sum, B_ROWS, True, sib_b, in0_b, in1_b, in2_b, sibsem_b, send_b, recv_b)
    sum_d = all_sum(d, d_sum, D_ROWS, False, sib_d, in0_d, in1_d, in2_d, sibsem_d, send_d, recv_d)

    pl.semaphore_wait(barrier, len(around))
    next(sum_a)
    next(sum_x)
    sent = [go(0), go(1)]
    next(sum_a)
    next(sum_x)
    for t in range(GROUP - 1, TURNS):
        turned(t)
    for n in range(GROUP + 1, TURNS):
        chosen = select(n)
        for t in range(GROUP, n):
            put_pair(b, B_ROWS, SECOND_ROW[t, n], at_columns(t, chosen))
    next(sum_b)
    next(sum_a)
    next(sum_x)
    next(sum_b)
    next(sum_a)
    next(sum_x)
    for n in range(GROUP, TURNS):
        chosen = select(n)
        for t in range(GROUP):
            cross[CROSS_AT[t, n]] = at_columns(t, chosen).astype(BF16)
    d[...] = jnp.zeros_like(d)
    next(sum_a)
    next(sum_x)
    sent += [go(2)]
    next(sum_b)
    next(sum_a)
    next(sum_b)
    next(sum_x, None)
    next(sum_a)
    sent += [go(3)]
    next(sum_a, None)

    def assimilate(t):
        left[t], change[t] = turn_operands(
            prior[t], values[pl.ds(order[t], 1), :], variances[pl.ds(order[t], 1), :])

    def first_prior(n):
        at = (n % 4) * 24
        for k in range(4):
            prior[n, k * SLAB:(k + 1) * SLAB, :] = x_all[n // 4, k, at:at + SLAB, :]

    for n in range(TURNS):
        first_prior(n)
    for t in range(GROUP):
        assimilate(t)
        for n in range(t + 1, TURNS):
            if n < GROUP:
                prior[n] += increment(prior[n], left[t], change[t], get_pair(a_sum, A_ROWS, FIRST_ROW[t, n]))
            else:
                at = (n - GROUP) * 2 * MEM
                step = increment(prior[n], left[t], change[t], cross[CROSS_AT[t, n]].astype(F32))
                d[at:at + MEM, :] += step[:, :LANES]
                d[at + MEM:at + 2 * MEM, :] += step[:, LANES:]
                prior[n] += step
    next(sum_d)
    next(sum_b)

    def turns(q, first, last):
        lanes = pl.ds(pl.multiple_of(q * CHUNK, 128), CHUNK)

        def turn(t, _):
            w_t = jnp.concatenate([wt[t, :, lanes].astype(F32)] * STACK, 1)
            x = state[q]
            state[q] = x + increment(x, left[t], change[t], w_t)
            return 0

        lax.fori_loop(first, last, turn, 0)

    def early(q):
        def level(s, _):
            lanes = pl.ds(pl.multiple_of(s * CHUNK, 128), CHUNK)
            for k in range(4):
                state[q, k * SLAB:(k + 1) * SLAB, lanes] = stage[k, q, pl.ds(s, SLAB, stride=STACK), :]
            return 0

        lax.fori_loop(0, STACK, level, 0)
        turns(q, 0, EARLY[q])

    next(sum_d)
    wait(sent[0])
    early(0)
    next(sum_d)
    next(sum_b)
    wait(sent[1])
    early(1)
    next(sum_d)
    next(sum_b)
    wait(sent[2])
    early(2)
    next(sum_d)
    next(sum_b, None)
    wait(sent[3])
    early(3)
    next(sum_d)
    next(sum_d, None)

    for n in range(GROUP, TURNS):
        first_prior(n)
        at = (n - GROUP) * 2 * MEM
        prior[n] += jnp.concatenate([d_sum[at:at + MEM, :], d_sum[at + MEM:at + 2 * MEM, :]], 1)
    for t in range(GROUP, TURNS):
        assimilate(t)
        for n in range(t + 1, TURNS):
            prior[n] += increment(prior[n], left[t], change[t], get_pair(b_sum, B_ROWS, SECOND_ROW[t, n]))

    def late(q, _):
        turns(q, jnp.where(q == 0, EARLY[0], EARLY[1]), TURNS)

        def level(s, _):
            lanes = pl.ds(pl.multiple_of(s * CHUNK, 128), CHUNK)
            for k in range(4):
                outbox[k, q, pl.ds(s, SLAB, stride=STACK), :] = state[q, k * SLAB:(k + 1) * SLAB, lanes]
            return 0

        lax.fori_loop(0, STACK, level, 0)
        started(back(q))
        return 0

    lax.fori_loop(0, CHUNKS, late, 0)
    for q in range(CHUNKS):
        wait(back(q))


def body(ensemble, loc_weight, obs_value, obs_var, owner_region, obs_cell, batch_order):
    flat = ensemble.reshape(SLAB * STACK, COLS_REG)
    smem, vmem, anywhere = (pl.BlockSpec(memory_space=m) for m in (pltpu.SMEM, pltpu.VMEM, pl.ANY))
    picked = pl.pallas_call(
        pick_kernel,
        out_shape=jax.ShapeDtypeStruct((TURNS, 24, OBS), F32),
        in_specs=[smem, smem, vmem, anywhere],
        out_specs=vmem,
        scratch_shapes=[
            pltpu.VMEM((4, SLAB * STACK, COLS_REG // 4), F32),
            pltpu.VMEM((3 * SLAB * STACK, COLS_REG // 4), BF16),
            pltpu.VMEM((TURNS, SLAB * STACK, OBS), F32),
            pltpu.SemaphoreType.DMA((4,)),
        ],
        compiler_params=pltpu.CompilerParams(vmem_limit_bytes=60 << 20),
        name="pick",
    )(batch_order, owner_region, obs_cell, flat)

    dma = pltpu.SemaphoreType.DMA

    def room(rows, twice):
        return [pltpu.VMEM((rows // 2, LANES), F32)] + [
            pltpu.VMEM((2, 3, rows // cut, LANES), F32) for cut in ((16, 64, 64) if twice else (16, 16, 16))]

    out = pl.pallas_call(
        main_kernel,
        out_shape=jax.ShapeDtypeStruct((SLAB * STACK, COLS_REG), F32),
        in_specs=[smem, smem, vmem, vmem, vmem, vmem, vmem, anywhere],
        out_specs=anywhere,
        scratch_shapes=[
            pltpu.VMEM((4, CHUNKS, SLAB * STACK, CHUNK), F32),
            pltpu.VMEM((4, CHUNKS, SLAB * STACK, CHUNK), F32),
            pltpu.VMEM((CHUNKS, MEM, CELLS), F32),
            pltpu.VMEM((TURNS, OBS, COLS_DEV), BF16),
            pltpu.VMEM((len(CROSS), OBS, OBS), BF16),
            pltpu.VMEM((TURNS, MEM, OBS), F32),
            pltpu.VMEM((TURNS, OBS, 3 * MEM), BF16),
            pltpu.VMEM((TURNS, 2 * MEM, OBS), BF16),
            *[pltpu.VMEM((rows, LANES), F32) for rows in (A_ROWS, A_ROWS, B_ROWS, B_ROWS, D_ROWS, D_ROWS)],
            *room(A_ROWS, True), *room(B_ROWS, True), *room(D_ROWS, False),
            pltpu.VMEM((X_ROWS, OBS), F32), pltpu.VMEM((2, 4, X_ROWS, OBS), F32), pltpu.VMEM((X_ROWS, OBS), F32),
            pltpu.VMEM((2, 3, X_ROWS // 2, OBS), F32), pltpu.VMEM((2, 3, X_ROWS // 2, OBS), F32),
            dma((CHUNKS, 3)), dma((CHUNKS, 3)), dma((CHUNKS,)),
            dma((CHUNKS, 3)), dma((CHUNKS, 3)), dma((CHUNKS,)),
            dma((4,)), dma((5, 2, 3)), dma((5, 2, 3)),
            dma((4,)), dma((5, 2, 3)), dma((5, 2, 3)),
            dma((4,)), dma((5, 2, 3)), dma((5, 2, 3)),
            dma((4,)), dma((3, 2, 3)), dma((3, 2, 3)),
        ],
        compiler_params=pltpu.CompilerParams(
            collective_id=0, has_side_effects=True, vmem_limit_bytes=60 << 20),
        name="filter",
    )(batch_order, owner_region, obs_cell, obs_value, obs_var, loc_weight,
      picked.reshape(TURNS * 24, OBS), flat)
    return out.reshape(SLAB, STACK, COLS_REG)


def solution(mesh):
    return jax.shard_map(
        body,
        mesh=mesh,
        in_specs=(P("grp", None, "region"), P(None, ("region", "grp"), None), P(), P(), P(), P(), P()),
        out_specs=P("grp", None, "region"),
        check_vma=False,
    )
```

time: 119 us -> 114 us (0.958)
  Pallas kernels: 115 us -> 110 us
    pallas_call x1, Pallas kernels: 114 us -> 109 us  [body(): pl.pallas_call(main_kernel, out_shape=jax.ShapeDtypeStruct((SLAB * STACK,...]
where the time goes in v3:
time: 114 us
  Pallas kernels  110 us (96%)
  local copies, waits for them, and re-layouts  3.53 us (3%)
    pallas_call x1, Pallas kernels, body(): pl.pallas_call(main_kernel, out_shape=jax.ShapeDtypeStruct((SLAB * STACK,...  109 us
    unnamed x1, local copies, waits for them, and re-layouts  3.53 us

profile of v3, /device:TPU:1, one launch (start us, length us, event | category | flops | bytes accessed | tf_op | source)
XLA Modules:
  0.0 113.6 jit_solution(17735134995269296795)
XLA Ops:
  0.0 1.4 %pick.1 = f32[8,24,256]{2,1,0:T(8,128)} custom-call(s32[8]{0:T(128)} %order.3, s32[8]{0:T(128)} %owner.3, s32[8,256]{1,0:T(8,128)} %cells.3, f32[320,2048]{1,0:T(8,128)} %bitcast.3), custom_call_target="tpu_custom_call" | custom-call | tf_op jit(solution)/shard_map/pick/pallas_call | solution.py:455
  1.4 108.6 %filter.1 = f32[320,2048]{1,0:T(8,128)} custom-call(s32[8]{0:T(128)} %order.3, s32[8]{0:T(128)} %owner.3, s32[8,256]{1,0:T(8,128)} %cells.3, f32[8,256]{1,0:T(8,128)} %values.1, f32[8,256]{1,0:T(8,128)} %variances.1, bf16[8,512,256]{2,1,0:T(8,128)(2,1)} %weights.1, f32[192,256]{1,0:T(8,128)} %bitcast.6, f32[320,2048]{1,0:T(8,128)} %bitcast.4), custom_call_target="tpu_custom_call" | custom-call | tf_op jit(solution)/shard_map/filter/pallas_call | solution.py:476
  110.0 3.5 %copy.9 = f32[20,16,2048]{2,1,0:T(8,128)} copy(f32[20,16,2048]{2,1,0:T(8,128)} %bitcast.5) | data formatting | bytes 5242880

commit v4 on v3

--- a/solution.py
+++ b/solution.py
@@ -26,6 +26,7 @@
 D_USED = 2 * (TURNS - GROUP) * MEM
 D_ROWS = -(-D_USED // 128) * 128
 X_ROWS = TURNS * 24 // 2
+PIECES = 2
 CHUNKS, CHUNK = 4, 128
 CELLS = STACK * CHUNK
 EARLY = [GROUP, GROUP - 1, GROUP - 1, GROUP - 1]
@@ -62,64 +63,6 @@
     left = jnp.concatenate([high, low, high], 0).T.astype(BF16)
     c_high, c_low = split2(change)
     return left, jnp.concatenate([c_high, c_low], 0)
-
-
-def pick_kernel(order, owner, cells, ens, out, held, pieces, total, sems):
-    here = lax.axis_index("region")
-    depth = COLS_REG // 4
-    out[...] = jnp.zeros_like(out)
-    some = functools.reduce(jnp.logical_or, [owner[order[t]] == here for t in range(TURNS)])
-
-    def columns_of(k):
-        return pl.ds(pl.multiple_of(k * depth, depth), depth)
-
-    def fetch(k):
-        return pltpu.make_async_copy(ens.at[:, columns_of(k)], held.at[k], sems.at[k])
-
-    def cell_of(t):
-        return cells[pl.ds(order[t], 1), :]
-
-    @pl.when(some)
-    def _():
-        for k in range(4):
-            fetch(k).start()
-
-        def part(k, _):
-            fetch(k).wait()
-            value = held[k]
-            high = value.astype(BF16)
-            middle, low = split2(value - high.astype(F32))
-            pieces[...] = jnp.concatenate([high, middle, low], 0)
-
-            def batch(t, _):
-                @pl.when(owner[order[t]] == here)
-                def _():
-                    column = cell_of(t) & (COLS_REG - 1)
-                    rows = lax.broadcasted_iota(jnp.int32, (depth, OBS), 0) + k * depth
-                    select = jnp.where(rows == column, 1.0, 0.0).astype(BF16)
-                    got = jnp.dot(pieces[...], select, preferred_element_type=F32)
-                    n = SLAB * STACK
-                    got = got[:n] + got[n:2 * n] + got[2 * n:]
-                    total[t] = jnp.where(k == 0, got, total[t] + got)
-
-                return 0
-
-            lax.fori_loop(0, TURNS, batch, 0)
-            return 0
-
-        lax.fori_loop(0, 4, part, 0)
-
-        def finish(t, _):
-            @pl.when(owner[order[t]] == here)
-            def _():
-                levels = lax.broadcasted_iota(jnp.int32, (SLAB, STACK, OBS), 1)
-                values = total[t].reshape(SLAB, STACK, OBS)
-                level = (cell_of(t) >> 11)[None]
-                out[t, 0:SLAB, :] = jnp.sum(jnp.where(levels == level, values, 0.0), 1)
-
-            return 0
-
-        lax.fori_loop(0, TURNS, finish, 0)
 
 
 def places():
@@ -263,19 +206,27 @@
     wait(copies)
 
 
-def main_kernel(order, owner, cells, values, variances, weights, picked, ens, out,
+def main_kernel(order_in, owner_in, cells_in, values_in, variances_in, weights_in, ens, out,
+                order, owner, cells, values, variances, weights, held, pieces, picked,
                 stage, outbox, state, wt, cross, prior, left, change,
                 a, a_sum, b, b_sum, d, d_sum, *rest):
     (sib_a, in0_a, in1_a, in2_a, sib_b, in0_b, in1_b, in2_b, sib_d, in0_d, in1_d, in2_d, x_half, x_all, sib_x, in0_x, in1_x,
      go_send, go_recv, go_own, back_send, back_recv, back_own,
      sibsem_a, send_a, recv_a, sibsem_b, send_b, recv_b, sibsem_d, send_d, recv_d,
-     sibsem_x, send_x, recv_x) = rest
+     sibsem_x, send_x, recv_x, in_sems, held_sems) = rest
     region, z = lax.axis_index("region"), lax.axis_index("grp")
 
     barrier = pltpu.get_barrier_semaphore()
     around = [peer(axis, k) for axis in ("x", "y", "z") for k in (1, 2, 3)] + [peer("c", 1)]
     for device in around:
         pl.semaphore_signal(barrier, 1, device_id=device, device_id_type=MESH)
+
+    arrays = ((order_in, order), (owner_in, owner), (cells_in, cells), (weights_in, weights),
+              (values_in, values), (variances_in, variances))
+    loads = started([pltpu.make_async_copy(src, dst, in_sems.at[i]) for i, (src, dst) in enumerate(arrays)])
+    blocks = started([
+        pltpu.make_async_copy(ens.at[:, k * COLS_DEV:(k + 1) * COLS_DEV], held.at[k], held_sems.at[k]) for k in range(4)])
+    wait(loads)
 
     def go(q):
         here = pl.ds(pl.multiple_of(z * COLS_DEV + q * CHUNK, 128), CHUNK)
@@ -324,38 +275,62 @@
     sum_b = all_sum(b, b_sum, B_ROWS, True, sib_b, in0_b, in1_b, in2_b, sibsem_b, send_b, recv_b)
     sum_d = all_sum(d, d_sum, D_ROWS, False, sib_d, in0_d, in1_d, in2_d, sibsem_d, send_d, recv_d)
 
+    def pick(n, _):
+        cell = cells[pl.ds(order[n], 1), :]
+        column = jnp.where(owner[order[n]] == region, cell & (COLS_REG - 1), -1)
+        total = jnp.zeros((SLAB * STACK, OBS), F32)
+        for k in range(4):
+            rows = lax.broadcasted_iota(jnp.int32, (COLS_DEV, OBS), 0) + k * COLS_DEV
+            chosen = jnp.where(rows == column, 1.0, 0.0).astype(BF16)
+            got = jnp.dot(pieces[k], chosen, preferred_element_type=F32)
+            for i in range(PIECES):
+                total = total + got[i * SLAB * STACK:(i + 1) * SLAB * STACK]
+        levels = lax.broadcasted_iota(jnp.int32, (SLAB, STACK, OBS), 1)
+        value = jnp.where(levels == (cell >> 11)[None], total.reshape(SLAB, STACK, OBS), 0.0)
+        picked[pl.ds(pl.multiple_of(n * 24, 8), SLAB), :] = jnp.sum(value, 1)
+        return 0
+
     pl.semaphore_wait(barrier, len(around))
     next(sum_a)
-    next(sum_x)
     sent = [go(0), go(1)]
-    next(sum_a)
+    picked[...] = jnp.zeros_like(picked)
+    for k in range(4):
+        wait(blocks[k:k + 1])
+        rest_of = held[k]
+        for i in range(PIECES):
+            piece = rest_of.astype(BF16)
+            pieces[k, i * SLAB * STACK:(i + 1) * SLAB * STACK, :] = piece
+            rest_of = rest_of - piece.astype(F32)
+    next(sum_a)
+    lax.fori_loop(0, 6, pick, 0)
+    next(sum_a)
+    lax.fori_loop(6, TURNS, pick, 0)
     next(sum_x)
     for t in range(GROUP - 1, TURNS):
         turned(t)
+    next(sum_x)
+    next(sum_a)
     for n in range(GROUP + 1, TURNS):
         chosen = select(n)
         for t in range(GROUP, n):
             put_pair(b, B_ROWS, SECOND_ROW[t, n], at_columns(t, chosen))
     next(sum_b)
-    next(sum_a)
     next(sum_x)
-    next(sum_b)
-    next(sum_a)
-    next(sum_x)
+    next(sum_a)
+    next(sum_b)
     for n in range(GROUP, TURNS):
         chosen = select(n)
         for t in range(GROUP):
             cross[CROSS_AT[t, n]] = at_columns(t, chosen).astype(BF16)
     d[...] = jnp.zeros_like(d)
-    next(sum_a)
+    next(sum_x)
+    next(sum_a)
+    next(sum_b)
     next(sum_x)
     sent += [go(2)]
-    next(sum_b)
     next(sum_a)
     next(sum_b)
     next(sum_x, None)
-    next(sum_a)
-    sent += [go(3)]
     next(sum_a, None)
 
     def assimilate(t):
@@ -381,7 +356,6 @@
                 d[at + MEM:at + 2 * MEM, :] += step[:, LANES:]
                 prior[n] += step
     next(sum_d)
-    next(sum_b)
 
     def turns(q, first, last):
         lanes = pl.ds(pl.multiple_of(q * CHUNK, 128), CHUNK)
@@ -405,21 +379,23 @@
         turns(q, 0, EARLY[q])
 
     next(sum_d)
+    next(sum_b)
+    sent += [go(3)]
     wait(sent[0])
     early(0)
     next(sum_d)
-    next(sum_b)
     wait(sent[1])
     early(1)
-    next(sum_d)
-    next(sum_b)
+    next(sum_b)
+    next(sum_d)
     wait(sent[2])
     early(2)
     next(sum_d)
-    next(sum_b, None)
+    next(sum_b)
     wait(sent[3])
     early(3)
     next(sum_d)
+    next(sum_b, None)
     next(sum_d, None)
 
     for n in range(GROUP, TURNS):
@@ -451,22 +427,6 @@
 
 def body(ensemble, loc_weight, obs_value, obs_var, owner_region, obs_cell, batch_order):
     flat = ensemble.reshape(SLAB * STACK, COLS_REG)
-    smem, vmem, anywhere = (pl.BlockSpec(memory_space=m) for m in (pltpu.SMEM, pltpu.VMEM, pl.ANY))
-    picked = pl.pallas_call(
-        pick_kernel,
-        out_shape=jax.ShapeDtypeStruct((TURNS, 24, OBS), F32),
-        in_specs=[smem, smem, vmem, anywhere],
-        out_specs=vmem,
-        scratch_shapes=[
-            pltpu.VMEM((4, SLAB * STACK, COLS_REG // 4), F32),
-            pltpu.VMEM((3 * SLAB * STACK, COLS_REG // 4), BF16),
-            pltpu.VMEM((TURNS, SLAB * STACK, OBS), F32),
-            pltpu.SemaphoreType.DMA((4,)),
-        ],
-        compiler_params=pltpu.CompilerParams(vmem_limit_bytes=60 << 20),
-        name="pick",
-    )(batch_order, owner_region, obs_cell, flat)
-
     dma = pltpu.SemaphoreType.DMA
 
     def room(rows, twice):
@@ -476,9 +436,15 @@
     out = pl.pallas_call(
         main_kernel,
         out_shape=jax.ShapeDtypeStruct((SLAB * STACK, COLS_REG), F32),
-        in_specs=[smem, smem, vmem, vmem, vmem, vmem, vmem, anywhere],
-        out_specs=anywhere,
+        in_specs=[pl.BlockSpec(memory_space=pltpu.HBM)] * 7,
+        out_specs=pl.BlockSpec(memory_space=pl.ANY),
         scratch_shapes=[
+            pltpu.SMEM((TURNS,), jnp.int32), pltpu.SMEM((TURNS,), jnp.int32), pltpu.VMEM((TURNS, OBS), jnp.int32),
+            pltpu.VMEM((TURNS, OBS), F32), pltpu.VMEM((TURNS, OBS), F32),
+            pltpu.VMEM((TURNS, COLS_DEV, OBS), BF16),
+            pltpu.VMEM((4, SLAB * STACK, COLS_DEV), F32),
+            pltpu.VMEM((4, PIECES * SLAB * STACK, COLS_DEV), BF16),
+            pltpu.VMEM((TURNS * 24, OBS), F32),
             pltpu.VMEM((4, CHUNKS, SLAB * STACK, CHUNK), F32),
             pltpu.VMEM((4, CHUNKS, SLAB * STACK, CHUNK), F32),
             pltpu.VMEM((CHUNKS, MEM, CELLS), F32),
@@ -497,12 +463,12 @@
             dma((4,)), dma((5, 2, 3)), dma((5, 2, 3)),
             dma((4,)), dma((5, 2, 3)), dma((5, 2, 3)),
             dma((4,)), dma((3, 2, 3)), dma((3, 2, 3)),
+            dma((6,)), dma((4,)),
         ],
         compiler_params=pltpu.CompilerParams(
             collective_id=0, has_side_effects=True, vmem_limit_bytes=60 << 20),
         name="filter",
-    )(batch_order, owner_region, obs_cell, obs_value, obs_var, loc_weight,
-      picked.reshape(TURNS * 24, OBS), flat)
+    )(batch_order, owner_region, obs_cell, obs_value, obs_var, loc_weight, flat)
     return out.reshape(SLAB, STACK, COLS_REG)
 
 

time: 114 us -> 107 us (0.939)
  Pallas kernels: 110 us -> 104 us
    pallas_call x1, Pallas kernels: 109 us -> 104 us  [body(): pl.pallas_call(main_kernel, out_shape=jax.ShapeDtypeStruct((SLAB * STACK,...]
    pallas_call x1 -> x0, Pallas kernels: 1.44 us -> none  [body(): pl.pallas_call(pick_kernel, out_shape=jax.ShapeDtypeStruct((TURNS, 24, OB...]
where the time goes in v4:
time: 107 us
  Pallas kernels  104 us (97%)
  local copies, waits for them, and re-layouts  3.53 us (3%)
    pallas_call x1, Pallas kernels, body(): pl.pallas_call(main_kernel, out_shape=jax.ShapeDtypeStruct((SLAB * STACK,...  104 us
    unnamed x1, local copies, waits for them, and re-layouts  3.53 us

profile of v4, /device:TPU:1, one launch (start us, length us, event | category | flops | bytes accessed | tf_op | source)
XLA Modules:
  0.0 107.2 jit_solution(7097428764489709335)
XLA Ops:
  0.0 103.7 %filter.1 = f32[320,2048]{1,0:T(8,128)} custom-call(s32[8]{0:T(128)} %order_in.1, s32[8]{0:T(128)} %owner_in.1, s32[8,256]{1,0:T(8,128)} %cells_in.1, f32[8,256]{1,0:T(8,128)} %values_in.1, f32[8,256]{1,0:T(8,128)} %variances_in.1, bf16[8,512,256]{2,1,0:T(8,128)(2,1)} %weights_in.1, f32[320,2048]{1,0:T(8,128)} %bitcast.3), custom_call_target="tpu_custom_call" | custom-call | tf_op jit(solution)/shard_map/filter/pallas_call | solution.py:436
  103.7 3.5 %copy.9 = f32[20,16,2048]{2,1,0:T(8,128)} copy(f32[20,16,2048]{2,1,0:T(8,128)} %bitcast.2) | data formatting | bytes 5242880

commit v5 on v4

--- a/solution.py
+++ b/solution.py
@@ -318,16 +318,16 @@
     next(sum_x)
     next(sum_a)
     next(sum_b)
+    next(sum_x)
+    next(sum_a)
     for n in range(GROUP, TURNS):
         chosen = select(n)
         for t in range(GROUP):
             cross[CROSS_AT[t, n]] = at_columns(t, chosen).astype(BF16)
     d[...] = jnp.zeros_like(d)
     next(sum_x)
-    next(sum_a)
-    next(sum_b)
-    next(sum_x)
     sent += [go(2)]
+    next(sum_b)
     next(sum_a)
     next(sum_b)
     next(sum_x, None)
@@ -357,16 +357,18 @@
                 prior[n] += step
     next(sum_d)
 
+    def turn(q, t):
+        lanes = pl.ds(pl.multiple_of(q * CHUNK, 128), CHUNK)
+        w_t = jnp.concatenate([wt[t, :, lanes].astype(F32)] * STACK, 1)
+        x = state[q]
+        state[q] = x + increment(x, left[t], change[t], w_t)
+
     def turns(q, first, last):
-        lanes = pl.ds(pl.multiple_of(q * CHUNK, 128), CHUNK)
-
-        def turn(t, _):
-            w_t = jnp.concatenate([wt[t, :, lanes].astype(F32)] * STACK, 1)
-            x = state[q]
-            state[q] = x + increment(x, left[t], change[t], w_t)
+        def one(t, _):
+            turn(q, t)
             return 0
 
-        lax.fori_loop(first, last, turn, 0)
+        lax.fori_loop(first, last, one, 0)
 
     def early(q):
         def level(s, _):
@@ -395,7 +397,6 @@
     wait(sent[3])
     early(3)
     next(sum_d)
-    next(sum_b, None)
     next(sum_d, None)
 
     for n in range(GROUP, TURNS):
@@ -404,12 +405,13 @@
         prior[n] += jnp.concatenate([d_sum[at:at + MEM, :], d_sum[at + MEM:at + 2 * MEM, :]], 1)
     for t in range(GROUP, TURNS):
         assimilate(t)
+        if t == GROUP:
+            next(sum_b, None)
         for n in range(t + 1, TURNS):
             prior[n] += increment(prior[n], left[t], change[t], get_pair(b_sum, B_ROWS, SECOND_ROW[t, n]))
-
-    def late(q, _):
-        turns(q, jnp.where(q == 0, EARLY[0], EARLY[1]), TURNS)
-
+        turn(0, t)
+
+    def give(q):
         def level(s, _):
             lanes = pl.ds(pl.multiple_of(s * CHUNK, 128), CHUNK)
             for k in range(4):
@@ -418,9 +420,14 @@
 
         lax.fori_loop(0, STACK, level, 0)
         started(back(q))
+
+    def late(q, _):
+        turns(q, EARLY[1], TURNS)
+        give(q)
         return 0
 
-    lax.fori_loop(0, CHUNKS, late, 0)
+    give(0)
+    lax.fori_loop(1, CHUNKS, late, 0)
     for q in range(CHUNKS):
         wait(back(q))
 

time: 107 us -> 107 us (level)
  no operation moved by 1% of the time
where the time goes in v5:
time: 107 us
  Pallas kernels  103 us (96%)
  local copies, waits for them, and re-layouts  3.53 us (3%)
    pallas_call x1, Pallas kernels, body(): pl.pallas_call(main_kernel, out_shape=jax.ShapeDtypeStruct((SLAB * STACK,...  103 us
    unnamed x1, local copies, waits for them, and re-layouts  3.53 us

profile of v5, /device:TPU:1, one launch (start us, length us, event | category | flops | bytes accessed | tf_op | source)
XLA Modules:
  0.0 106.5 jit_solution(7100816791163052762)
XLA Ops:
  0.0 103.0 %filter.1 = f32[320,2048]{1,0:T(8,128)} custom-call(s32[8]{0:T(128)} %order_in.1, s32[8]{0:T(128)} %owner_in.1, s32[8,256]{1,0:T(8,128)} %cells_in.1, f32[8,256]{1,0:T(8,128)} %values_in.1, f32[8,256]{1,0:T(8,128)} %variances_in.1, bf16[8,512,256]{2,1,0:T(8,128)(2,1)} %weights_in.1, f32[320,2048]{1,0:T(8,128)} %bitcast.3), custom_call_target="tpu_custom_call" | custom-call | tf_op jit(solution)/shard_map/filter/pallas_call | solution.py:443
  103.0 3.5 %copy.9 = f32[20,16,2048]{2,1,0:T(8,128)} copy(f32[20,16,2048]{2,1,0:T(8,128)} %bitcast.2) | data formatting | bytes 5242880

commit v6 on v5

--- a/solution.py
+++ b/solution.py
@@ -246,7 +246,7 @@
         return copies
 
     def turned(t):
-        wt[t] = weights[order[t]].astype(F32).T.astype(BF16)
+        wt[t] = weights[order[t]].T
 
     def select(n):
         column = cells[pl.ds(order[n], 1), :] & (COLS_REG - 1)

time: 107 us -> 107 us (level)
  no operation moved by 1% of the time
where the time goes in v6:
time: 107 us; the launch traced here: 106 us
  Pallas kernels  103 us (96%)
  local copies, waits for them, and re-layouts  3.53 us (3%)
    pallas_call x1, Pallas kernels, body(): pl.pallas_call(main_kernel, out_shape=jax.ShapeDtypeStruct((SLAB * STACK,...  103 us
    unnamed x1, local copies, waits for them, and re-layouts  3.53 us

profile of v6, /device:TPU:1, one launch (start us, length us, event | category | flops | bytes accessed | tf_op | source)
XLA Modules:
  0.0 106.5 jit_solution(17686009151617580711)
XLA Ops:
  0.0 103.0 %filter.1 = f32[320,2048]{1,0:T(8,128)} custom-call(s32[8]{0:T(128)} %order_in.1, s32[8]{0:T(128)} %owner_in.1, s32[8,256]{1,0:T(8,128)} %cells_in.1, f32[8,256]{1,0:T(8,128)} %values_in.1, f32[8,256]{1,0:T(8,128)} %variances_in.1, bf16[8,512,256]{2,1,0:T(8,128)(2,1)} %weights_in.1, f32[320,2048]{1,0:T(8,128)} %bitcast.3), custom_call_target="tpu_custom_call" | custom-call | tf_op jit(solution)/shard_map/filter/pallas_call | solution.py:443
  103.0 3.5 %copy.9 = f32[20,16,2048]{2,1,0:T(8,128)} copy(f32[20,16,2048]{2,1,0:T(8,128)} %bitcast.2) | data formatting | bytes 5242880
